TPU v7x, 512 devices: a whole 4x4x16 slice. The times are simulated.
512 devices in a mesh: groups: 8 (over x, core), owners: 64 (over y, z).
Axes of the slice: x: 4, y: 4, z: 16, core: 2. Of those that a mesh axis runs over, the one named last changes fastest.
Arguments:
- vectors: bfloat16 [65536, 768], P(('groups', 'owners')), may hold values from -6 to 6
- list_ids: int32 [65536], P(('groups', 'owners')), may hold values from 0 to 65535, as said below
- codes: int32 [192, 65536], P(None, ('groups', 'owners')), may hold values from 0 to 255
- centroids: bfloat16 [65536, 768], P(('groups', 'owners')), may hold values from -5 to 5
- codebook0: float32 [96, 8, 256], replicated, may hold values from -6 to 6
Outputs:
- codebook: float32 [96, 8, 256], replicated
- list_error: float32 [65536], P(('groups', 'owners'))
Inputs may be any that keep to these rules, and one draw needn't show every extreme that they name: `list_ids`: the owner index of list l is (l // 128) % 64. Among the 128 vectors of one device at most 6 lie in lists of one owner index; in each group of 64 consecutive devices one owner index gets exactly 6 vectors from every device of the group.
All inputs are finite; a program needn't handle non-finite values.
Results may differ from a plain program's by a relative error of at most 0.0003.
Values may be sent and summed in bfloat16 or wider, within the bound.
A program may use at most 128 MiB of HBM per device.

v0:
```python
import jax
import jax.numpy as jnp
from jax import lax
from jax.sharding import PartitionSpec as P


def block_rows():
    return 128


def code_totals_local(residual, codes, weight, sub_count, code_count):
    rows_here, feat_dim = residual.shape
    sub_width = feat_dim // sub_count
    step_rows = block_rows()
    block_count = rows_here // step_rows
    pieces = residual.reshape(block_count, step_rows, sub_count, sub_width)
    code_blocks = codes.reshape(block_count, step_rows, 2 * sub_count)
    weight_blocks = weight.reshape(block_count, step_rows)
    levels = jnp.arange(code_count, dtype=jnp.int32)

    def add_block(carry, block):
        piece, block_codes, block_weight = block
        sum_list = []
        count_list = []
        for which_refit in range(2):
            chosen = block_codes[:, which_refit * sub_count : (which_refit + 1) * sub_count]
            onehot = (chosen[:, :, None] == levels[None, None, :]).astype(jnp.float32)
            sum_list.append(
                jnp.einsum("rmk,rmd->mkd", onehot, piece, precision=lax.Precision.HIGHEST)
            )
            count_list.append(
                jnp.einsum("rmk,r->mk", onehot, block_weight, precision=lax.Precision.HIGHEST)
            )
        return ((carry[0] + jnp.stack(sum_list), carry[1] + jnp.stack(count_list)), None)

    start = (
        jnp.zeros((2, sub_count, code_count, sub_width), jnp.float32),
        jnp.zeros((2, sub_count, code_count), jnp.float32),
    )
    (sums, counts), _ = lax.scan(add_block, start, (pieces, code_blocks, weight_blocks))
    return (
        sums.reshape(2, sub_count * code_count, sub_width),
        counts.reshape(2, sub_count * code_count),
    )


def refit_pair(code_sums, code_counts, start_book, prior_weight):
    first_book = (code_sums[0] + prior_weight * start_book) / (
        code_counts[0][:, None] + prior_weight
    )
    return (code_sums[1] + prior_weight * first_book) / (code_counts[1][:, None] + prior_weight)


def vector_errors(residual, codes, book_flat, sub_count, code_count):
    rows_here, feat_dim = residual.shape
    sub_width = feat_dim // sub_count
    step_rows = block_rows()
    block_count = rows_here // step_rows
    book = book_flat.reshape(sub_count, code_count, sub_width)
    pieces = residual.reshape(block_count, step_rows, sub_count, sub_width)
    code_blocks = codes[:, sub_count : 2 * sub_count].reshape(block_count, step_rows, sub_count)
    levels = jnp.arange(code_count, dtype=jnp.int32)

    def one_block(carry, block):
        piece, chosen = block
        onehot = (chosen[:, :, None] == levels[None, None, :]).astype(jnp.float32)
        recon = jnp.einsum("rmk,mkd->rmd", onehot, book, precision=lax.Precision.HIGHEST)
        diff = piece - recon
        return (carry, jnp.sum(diff * diff, axis=(1, 2)) / feat_dim)

    _, errors = lax.scan(one_block, 0.0, (pieces, code_blocks))
    return errors.reshape(rows_here)


def local(vectors, list_ids, codes, centroids, codebook0):
    owner_count = lax.axis_size("owners")
    device_count = lax.axis_size("groups") * owner_count
    vec_rows, feat_dim = vectors.shape
    list_rows = centroids.shape[0]
    sub_count, sub_width, code_count = codebook0.shape
    capacity = 3 * vec_rows // owner_count
    slot_total = owner_count * capacity
    prior_weight = float(vec_rows * device_count // (2 * code_count))
    code_rows = codes.T
    owned_rows = lax.all_gather(centroids, "groups", axis=0, tiled=True)
    list_total = owned_rows.shape[0]
    owner_ids = list_ids // list_rows % owner_count
    local_list = list_ids // (list_rows * owner_count) * list_rows + list_ids % list_rows
    matches = (owner_ids[:, None] == jnp.arange(owner_count, dtype=jnp.int32)[None, :]).astype(
        jnp.int32
    )
    slot_rank = jnp.sum(jnp.cumsum(matches, axis=0) * matches, axis=1) - 1
    slot_index = owner_ids * capacity + slot_rank
    slot_list = (
        jnp.full((slot_total,), -1, jnp.int32)
        .at[slot_index]
        .set(local_list)
        .reshape(owner_count, capacity)
    )
    code_cols = code_rows.shape[1]
    slot_rows = (
        jnp.zeros((slot_total, feat_dim), jnp.bfloat16)
        .at[slot_index]
        .set(vectors)
        .reshape(owner_count, capacity, feat_dim)
    )
    slot_codes = (
        jnp.zeros((slot_total, code_cols), jnp.int32)
        .at[slot_index]
        .set(code_rows)
        .reshape(owner_count, capacity, code_cols)
    )
    got_rows, got_codes, held_list = (
        lax.all_to_all(slot_rows, "owners", split_axis=0, concat_axis=0, tiled=True),
        lax.all_to_all(slot_codes, "owners", split_axis=0, concat_axis=0, tiled=True),
        lax.all_to_all(slot_list, "owners", split_axis=0, concat_axis=0, tiled=True),
    )
    held_flat_list = held_list.reshape(slot_total)
    filled = held_flat_list >= 0
    base_rows = jnp.take(owned_rows, jnp.clip(held_flat_list, 0, list_total - 1), axis=0)
    residual = jnp.where(
        filled[:, None],
        got_rows.reshape(slot_total, feat_dim).astype(jnp.float32) - base_rows.astype(jnp.float32),
        0.0,
    )
    held_codes = got_codes.reshape(slot_total, code_cols)
    code_sums, code_counts = code_totals_local(
        residual, held_codes, filled.astype(jnp.float32), sub_count, code_count
    )
    start_book = jnp.transpose(codebook0, (0, 2, 1)).reshape(sub_count * code_count, sub_width)
    code_sums, code_counts = lax.psum((code_sums, code_counts), ("groups", "owners"))
    book_flat = refit_pair(code_sums, code_counts, start_book, prior_weight)
    errors = vector_errors(residual, held_codes, book_flat, sub_count, code_count)
    got_errors = jnp.where(filled, errors, 0.0)
    held_targets = jnp.clip(held_list.reshape(slot_total), 0, list_total - 1)
    per_list = jax.ops.segment_sum(got_errors, held_targets, list_total)
    list_error = lax.psum_scatter(per_list, "groups", scatter_dimension=0, tiled=True)
    codebook = jnp.transpose(book_flat.reshape(sub_count, code_count, sub_width), (0, 2, 1))
    return (codebook, list_error)


def solution(mesh):
    in_specs = (
        P(("groups", "owners"), None),
        P(("groups", "owners")),
        P(None, ("groups", "owners")),
        P(("groups", "owners"), None),
        P(),
    )
    out_specs = (P(), P(("groups", "owners")))
    return jax.shard_map(local, mesh=mesh, in_specs=in_specs, out_specs=out_specs, check_vma=False)
```

profile of v0, /device:TPU:1, one launch (start us, length us, event | category | flops | bytes accessed | tf_op | source)
XLA Modules:
  0.0 782.1 jit_solution(12604098772163085204)
XLA Ops:
  7.2 0.7 fusion.45
  7.9 0.2 reduce_window_sum.11
  8.1 0.2 select_reduce_fusion
  8.3 1.0 scatter_custom_fusion.1
  9.3 0.8 all_to_all.13
  10.0 19.3 %all-to-all-start.1 = ((s32[64,1,6]{2,1,0:T(1,128)}), s32[64,1,6]{2,1,0:T(1,128)S(1)}, u32[]{:S(2)}, u32[]{:S(2)}) async-start(s32[64,1,6]{2,1,0:T(1,128)} %bitcast.1), calls=%async_computation.1 | async-start | bytes 65536 | tf_op jit(solution)/shard_map/all_to_all | solution.py:116
  29.3 1.0 copy.17
  30.3 1.1 scatter_custom_fusion
  31.4 0.8 reshape.149
  32.3 10.3 %all-to-all-done.1 = s32[64,1,6]{2,1,0:T(1,128)S(1)} async-done(((s32[64,1,6]{2,1,0:T(1,128)}), s32[64,1,6]{2,1,0:T(1,128)S(1)}, u32[]{:S(2)}, u32[]{:S(2)}) %all-to-all-start.1) | async-done | bytes 1568 | tf_op jit(solution)/shard_map/all_to_all | solution.py:116
  42.5 4.6 all-to-all-start
  47.2 0.7 all-gather.2.cloned.1.call-update
  47.9 1.7 scatter_custom_fusion.2
  49.6 1.1 reshape.150
  50.7 24.5 %all-to-all-done = s32[64,6,192]{2,1,0:T(8,128)S(1)} async-done(((s32[64,6,192]{2,1,0:T(8,128)}), s32[64,6,192]{2,1,0:T(8,128)S(1)}, u32[]{:S(2)}, u32[]{:S(2)}) %all-to-all-start) | async-done | bytes 294944 | tf_op jit(solution)/shard_map/all_to_all | solution.py:115
  75.2 9.6 %all-to-all-start.2 = ((bf16[64,6,768]{2,1,0:T(8,128)(2,1)}), bf16[64,6,768]{2,1,0:T(8,128)(2,1)S(1)}, u32[]{:S(2)}, u32[]{:S(2)}) async-start(bf16[64,6,768]{2,1,0:T(8,128)(2,1)} %reshape.150), calls=%async_computation.2 | async-start | bytes 1572864 | tf_op jit(solution)/shard_map/all_to_all | solution.py:114
  85.0 0.1 min.20
  85.3 0.1 ge.33
  85.4 0.1 min.18
  85.6 0.8 reshape_reshape.3
  86.4 1.9 copy.21
  88.3 35.0 %all-to-all-done.2 = bf16[64,6,768]{2,1,0:T(8,128)(2,1)S(1)} async-done(((bf16[64,6,768]{2,1,0:T(8,128)(2,1)}), bf16[64,6,768]{2,1,0:T(8,128)(2,1)S(1)}, u32[]{:S(2)}, u32[]{:S(2)}) %all-to-all-start.2) | async-done | bytes 589856 | tf_op jit(solution)/shard_map/all_to_all | solution.py:114
  123.3 12.5 %reshape.156 = f32[3,128,96,8]{3,2,1,0:T(8,128)} reshape(bf16[64,6,768]{2,1,0:T(8,128)(2,1)S(1)} %all-to-all-done.2) | data formatting | bytes 1769472 | tf_op jit(solution)/shard_map/convert_element_type | solution.py:123
  135.7 4.1 gather_fusion
  139.9 12.1 %reshape.205 = bf16[3,128,96,8]{3,2,1,0:T(8,128)(2,1)} reshape(bf16[384,768]{1,0:T(8,128)(2,1)S(1)} %gather_fusion) | data formatting | bytes 1179648 | tf_op jit(solution)/shard_map/jit(_take)/gather | solution.py:120
  151.9 17.6 %subtract_select_fusion = f32[3,128,96,8]{3,2,1,0:T(8,128)} fusion(f32[3,128,96,8]{3,2,1,0:T(8,128)} %reshape.156, bf16[3,128,96,8]{3,2,1,0:T(8,128)(2,1)} %reshape.205, pred[3,128]{1,0:T(4,128)(4,1)S(1)} %compare_and_fusion, pred[3,128]{1,0:T(4,128)(4,1)S(1)} %ge.33), kind=kLoop, calls=%fused_computation.39 | loop fusion | flops 1179648 | bytes 2949888 | tf_op jit(solution)/shard_map/jit(_where)/select_n | solution.py:121
  169.5 14.4 %copy.22 = f32[3,128,96,8]{1,3,2,0:T(8,128)} copy(f32[3,128,96,8]{3,2,1,0:T(8,128)} %subtract_select_fusion) | data formatting | bytes 2359296
  183.9 76.2 %while.26 = (s32[]{:T(128)}, f32[2,96,256,8]{2,3,1,0:T(8,128)S(1)}, f32[2,96,256]{2,1,0:T(8,128)S(1)}, s32[3,128,192]{1,2,0:T(8,128)}, f32[3,128,96,8]{1,3,2,0:T...) while((s32[]{:T(128)}, f32[2,96,256,8]{2,3,1,0:T(8,128)S(1)}, ...), condition=%wide.region_6.7_spmd.clone.clone, body=%wide.region_5.6_spmd.clone.clone.sunk | while | flops 693387264 | bytes 8849516 | solution.py:40
  183.9 0.9 dynamic-slice_bitcast_fusion.5
  184.8 6.4 fusion.69
  191.3 6.4 fusion.70
  197.7 0.4 maximum_add_fusion.4
  198.2 5.5 fusion.71
  203.7 5.5 fusion.72
  209.3 0.9 dynamic-slice_bitcast_fusion.5
  210.2 6.4 fusion.69
  216.7 6.4 fusion.70
  223.1 0.4 maximum_add_fusion.4
  223.6 5.5 fusion.71
  229.1 5.5 fusion.72
  234.7 0.9 dynamic-slice_bitcast_fusion.5
  235.6 6.4 fusion.69
  242.1 6.4 fusion.70
  248.5 0.4 maximum_add_fusion.4
  249.0 5.5 fusion.71
  254.5 5.5 fusion.72
  260.1 1.0 copy.30
  261.1 0.2 copy-done
  261.4 1.4 dynamic-slice
  263.5 0.1 ge.37
  263.6 0.1 reshape.191
  263.8 1.1 reshape.153
  265.0 0.1 copy.25
  265.1 467.4 %all-reduce.4.cloned.1.call-done = (f32[2,24576,8]{1,2,0:T(8,128)}, f32[2,24576]{1,0:T(2,128)}) async-done(((f32[2,24576,8]{1,2,0:T(8,128)}, f32[2,24576]{1,0:T(2,128)}), (f32[2,24576,8]{1,2,0:T(8,128)}, f32[2,24576]{1,0:T(2,128)})) %all-reduce.4.cloned.1.call-update) | async-done | bytes 1769488 | tf_op jit(solution)/shard_map/psum | solution.py:131
  732.5 1.5 fusion.49
  734.0 0.6 fusion.38
  734.7 0.3 fusion.32
  734.9 23.5 %while.25 = (s32[]{:T(128)}, f32[3,128]{1,0:T(4,128)S(1)}, f32[3,128,96,8]{1,3,2,0:T(8,128)}, s32[3,128,96]{1,2,0:T(8,128)S(1)}, f32[96,256,8]{1,2,0:T(8,128)S(1)}, /*index=5*/s32[]{:T(128)}, s32[]{:T(128)}) while((s32[]{:T(128)}, f32[3,128]{1,0:T(4,128)S(1)}, f32[3,128,96,8]{1,3,2,0:T(8,128)}, s32[3,128,96]{1,2,0:T(8,128)S(1)}, ...), condition=%wide.region_11.12_spmd.clone, body=%wide.region_9.11_spmd.clone.sunk | while | flops 305430528 | bytes 1329753 | solution.py:71
  735.0 7.7 fusion.63
  742.8 7.7 fusion.63
  750.6 7.7 fusion.63
  758.4 3.9 scatter_custom_fusion.3
  762.3 12.3 %all-reduce = f32[1024]{0:T(1024)S(1)} all-reduce(f32[1024]{0:T(1024)S(1)} %scatter_custom_fusion.3), channel_id=2, replica_groups=mesh['groups'=8,'owners'=64] {'groups'}, use_global_device_ids=true, to_apply=%region_13.14.clone | all-reduce | flops 1024 | bytes 8192
  774.7 0.6 dynamic-slice.1
  (49 shorter events, 1.1 us)
Async XLA Ops:
  10.0 32.5 %all-to-all-start.1 = ((s32[64,1,6]{2,1,0:T(1,128)}), s32[64,1,6]{2,1,0:T(1,128)S(1)}, u32[]{:S(2)}, u32[]{:S(2)}) async-start(s32[64,1,6]{2,1,0:T(1,128)} %bitcast.1), calls=%async_computation.1 | async-start | bytes 65536 | tf_op jit(solution)/shard_map/all_to_all | solution.py:116
  42.5 32.7 %all-to-all-start = ((s32[64,6,192]{2,1,0:T(8,128)}), s32[64,6,192]{2,1,0:T(8,128)S(1)}, u32[]{:S(2)}, u32[]{:S(2)}) async-start(s32[64,6,192]{2,1,0:T(8,128)} %reshape.149), calls=%async_computation | async-start | bytes 1048576 | tf_op jit(solution)/shard_map/all_to_all | solution.py:115
  47.2 88.6 %all-gather.2.cloned.1.call-start = ((), (), s32[]{:S(2)}) async-start(), calls=%async_computation.3 | async-start | bytes 1769472 | tf_op jit(solution)/shard_map/all_gather | solution.py:85
  75.2 60.5 %copy-start.1 = (s32[64,6,192]{2,1,0:T(8,128)}, s32[64,6,192]{2,1,0:T(8,128)S(1)}, u32[]{:S(2)}) copy-start(s32[64,6,192]{2,1,0:T(8,128)S(1)} %all-to-all-done) | copy-start | bytes 884740
  75.2 48.0 %all-to-all-start.2 = ((bf16[64,6,768]{2,1,0:T(8,128)(2,1)}), bf16[64,6,768]{2,1,0:T(8,128)(2,1)S(1)}, u32[]{:S(2)}, u32[]{:S(2)}) async-start(bf16[64,6,768]{2,1,0:T(8,128)(2,1)} %reshape.150), calls=%async_computation.2 | async-start | bytes 1572864 | tf_op jit(solution)/shard_map/all_to_all | solution.py:114
  84.8 647.7 %all-reduce.4.cloned.1.call-start = ((), (), s32[]{:S(2)}) async-start(), calls=%async_computation.4 | async-start | bytes 3538944 | tf_op jit(solution)/shard_map/psum | solution.py:131
  260.1 1.2 copy-start
  261.3 473.3 %copy-start.2 = (f32[96,8,256]{2,1,0:T(8,128)S(1)}, f32[96,8,256]{2,1,0:T(8,128)}, u32[]{:S(2)}) copy-start(f32[96,8,256]{2,1,0:T(8,128)} %param.13) | copy-start | bytes 2359300
  732.5 1.5 copy-start.4
  758.4 16.8 %copy-start.3 = (f32[96,256,8]{1,2,0:T(8,128)}, f32[96,256,8]{1,2,0:T(8,128)S(1)}, u32[]{:S(2)}) copy-start(f32[96,256,8]{1,2,0:T(8,128)S(1)} %get-tuple-element.318) | copy-start | bytes 2359300
Sparse Core Ops, SparseCore 0:
  50.1 34.8 all-gather.1
  261.5 470.9 all-reduce.3
where the time goes:
time: 786 us; the launch traced here: 782 us
  waiting for transfers between devices  538 us (68%)
  matrix products  94.9 us (12%)
  local copies, waits for them, and re-layouts  62.9 us (8%)
  starting transfers between devices  33.6 us (4%)
  other arithmetic  25.2 us (3%)
  between operations  15 us (2%)
  blocking collectives  12.3 us (2%)
    psum x1, waiting for transfers between devices, local(): lax.psum((code_sums, code_counts), ('groups', 'owners'))  467 us
    dot_general x6, matrix products, add_block(): jnp.einsum('rmk,rmd->mkd', onehot, piece, precision=lax.Precision.HIGHEST)  38.6 us
    all_to_all x1, waiting for transfers between devices, local(): lax.all_to_all(slot_rows, 'owners', split_axis=0, concat_axis=0, tiled=True)  35 us
    dot_general x6, matrix products, add_block(): jnp.einsum('rmk,r->mk', onehot, block_weight, precision=lax.Precision.HIG...  33.1 us
    all_to_all x1, waiting for transfers between devices, local(): lax.all_to_all(slot_codes, 'owners', split_axis=0, concat_axis=0, tiled=T...  24.5 us
    dot_general x3, matrix products, one_block(): jnp.einsum('rmk,mkd->rmd', onehot, book, precision=lax.Precision.HIGHEST)  23.2 us
    unnamed x16, local copies, waits for them, and re-layouts  19.6 us
    all_to_all x1, starting transfers between devices, local(): lax.all_to_all(slot_list, 'owners', split_axis=0, concat_axis=0, tiled=True)  19.3 us
  transfers between devices with their start and end apart: 5, of which 4 were waited for; matrix products, arithmetic and copies ran while one was open for 3% of the time, Pallas kernels for 0%

commit v1 on v0

v1 whole, which is shorter than its diff:
```python
import functools

import jax
import jax.numpy as jnp
from jax import lax
from jax.experimental import pallas as pl
from jax.experimental.pallas import tpu as pltpu
from jax.sharding import PartitionSpec as P

MESH = pl.DeviceIdType.MESH
F32 = jnp.float32
BF16 = jnp.bfloat16
I32 = jnp.int32

ROWS = 128
DIM = 768
SUBS = 96
WIDTH = 8
CODES = 256
OWNERS = 64
GROUPS = 8
CAP = 6
SLOTS = 8
LANES = 128
PAIRS = 3
LISTS_HERE = GROUPS * ROWS
CHUNKS = 32
CHUNK_SUBS = SUBS // CHUNKS
CHUNK_ROWS = 56
PLANE = 16
PRIOR = 128.0
UNIT_PLACES = (0, 2, 5, 8, 10, 13)
VMEM_LIMIT = 48 * 1024 * 1024


def vmem():
    return pl.BlockSpec(memory_space=pltpu.VMEM)


def wait_bytes(ref, sem):
    pltpu.make_async_copy(ref, ref, sem).wait()


def place():
    group, owner = lax.axis_index("groups"), lax.axis_index("owners")
    return group, owner


def fetch_kernel(ids_ref, cent_ref, rows_ref, key_ref, ids_all, table, sendbuf, id_send, id_recv,
                 own_sem, x_send, x_recv, sib_send, sib_recv, row_send, row_recv):
    group, owner = place()
    y, z = owner // 16, owner % 16
    sibling = group + 1 - 2 * (group % 2)

    barrier = pltpu.get_barrier_semaphore()

    def greet(k, _):
        pl.semaphore_signal(barrier, inc=1, device_id=(group, (owner + k) % OWNERS), device_id_type=MESH)
        return 0

    lax.fori_loop(1, OWNERS, greet, 0)
    for k in range(1, GROUPS):
        pl.semaphore_signal(barrier, inc=1, device_id=((group + k) % GROUPS, owner), device_id_type=MESH)
    pl.semaphore_wait(barrier, OWNERS - 1 + GROUPS - 1)

    def id_copy(k):
        return pltpu.make_async_remote_copy(
            ids_ref, ids_all.at[owner], id_send, id_recv, device_id=(group, (owner + k) % OWNERS), device_id_type=MESH)

    own = pltpu.make_async_copy(cent_ref, table.at[group], own_sem)
    own.start()
    across = []
    for j in range(1, 4):
        across.append(pltpu.make_async_remote_copy(
            cent_ref, table.at[group], x_send.at[j - 1], x_recv.at[j - 1],
            device_id=((group + 2 * j) % GROUPS, owner), device_id_type=MESH))
    lax.fori_loop(1, OWNERS, lambda k, _: (id_copy(k).start(), 0)[1], 0)
    for copy in across:
        copy.start()
    aside = [pltpu.make_async_remote_copy(
        cent_ref, table.at[group], sib_send.at[0], sib_recv.at[0], device_id=(sibling, owner), device_id_type=MESH)]
    aside[0].start()
    ids_all[owner] = ids_ref[...]

    wait_bytes(ids_all.at[pl.ds(0, OWNERS - 1)], id_recv)
    ids = ids_all[:, 0, :]
    mine = ((ids >> 7) & (OWNERS - 1)) == owner
    before = (lax.broadcasted_iota(I32, (LANES, LANES), 0) < lax.broadcasted_iota(I32, (LANES, LANES), 1))
    rank = jnp.dot(mine.astype(F32).astype(BF16), before.astype(F32).astype(BF16), preferred_element_type=F32)
    local = (((ids >> 13) << 7) + (ids & 127) + 1).astype(F32)
    key = jnp.where(mine, rank * 2048.0 + local, -1.0)
    key_ref[:, 0, :] = key

    for j in range(1, 4):
        source = (group + 2 * GROUPS - 2 * j) % GROUPS
        across[j - 1].wait_recv()
        relay = pltpu.make_async_remote_copy(
            table.at[source], table.at[source], sib_send.at[j], sib_recv.at[j],
            device_id=(sibling, owner), device_id_type=MESH)
        relay.start()
        aside.append(relay)
    own.wait()
    for copy in aside:
        copy.wait_recv()

    lists = table[...].reshape(LISTS_HERE, DIM)
    list_lane = lax.broadcasted_iota(I32, (16, SLOTS, LISTS_HERE), 2).astype(F32) + 1.0
    slot_base = lax.broadcasted_iota(I32, (16, SLOTS, LANES), 1).astype(F32) * 2048.0

    def row_copy(peer):
        return pltpu.make_async_remote_copy(
            sendbuf.at[peer], rows_ref.at[owner], row_send, row_recv, device_id=(group, peer), device_id_type=MESH)

    def serve(q, _):
        first = ((y + q) % 4) * 16
        at = key_ref[pl.ds(first, 16)] - slot_base
        hit = (at > 0.5) & (at < 1024.5)
        which = jnp.sum(jnp.where(hit, at, 0.0), axis=2, keepdims=True)
        pick = (which == list_lane).astype(F32).reshape(16 * SLOTS, LISTS_HERE).astype(BF16)
        got = jnp.dot(pick, lists, preferred_element_type=F32).reshape(16, SLOTS, DIM)
        for p in range(PAIRS):
            both = jnp.concatenate(
                [got[:, :, 256 * p: 256 * p + 128], got[:, :, 256 * p + 128: 256 * p + 256]], axis=1)
            sendbuf[pl.ds(first, 16), 16 * p: 16 * p + 16, :] = both.astype(BF16)

        def send(k, _):
            peer = first + (z + k) % 16

            @pl.when(peer != owner)
            def _():
                row_copy(peer).start()
            return 0

        lax.fori_loop(0, 16, send, 0)
        return 0

    lax.fori_loop(0, 4, serve, 0)
    rows_ref[owner] = sendbuf[owner]

    for copy in across + aside:
        copy.wait_send()
    wait_bytes(ids_all.at[pl.ds(0, OWNERS - 1)], id_send)
    wait_bytes(sendbuf.at[pl.ds(0, OWNERS - 1)], row_send)
    wait_bytes(sendbuf.at[pl.ds(0, OWNERS - 1)], row_recv)


def fetch_rows(ids_row, centroids):
    return pl.pallas_call(
        fetch_kernel,
        out_shape=(jax.ShapeDtypeStruct((OWNERS, 16 * PAIRS, LANES), BF16),
                   jax.ShapeDtypeStruct((OWNERS, 1, LANES), F32)),
        in_specs=[vmem()] * 2,
        out_specs=(vmem(), vmem()),
        scratch_shapes=[
            pltpu.VMEM((OWNERS, 1, LANES), I32),
            pltpu.VMEM((GROUPS, ROWS, DIM), BF16),
            pltpu.VMEM((OWNERS, 16 * PAIRS, LANES), BF16),
            pltpu.SemaphoreType.DMA, pltpu.SemaphoreType.DMA, pltpu.SemaphoreType.DMA,
            pltpu.SemaphoreType.DMA((3,)), pltpu.SemaphoreType.DMA((3,)),
            pltpu.SemaphoreType.DMA((4,)), pltpu.SemaphoreType.DMA((4,)),
            pltpu.SemaphoreType.DMA, pltpu.SemaphoreType.DMA,
        ],
        compiler_params=pltpu.CompilerParams(collective_id=0, has_side_effects=True, vmem_limit_bytes=VMEM_LIMIT),
    )(ids_row, centroids)


def totals_kernel(ids_ref, rows_ref, vec_ref, codes_ref, sums_ref, resid_ref, stacked):
    ids = ids_ref[...]
    owner = (ids >> 7) & (OWNERS - 1)
    in_owner = (lax.broadcasted_iota(I32, (OWNERS, LANES), 0) == owner).astype(F32)
    before = (lax.broadcasted_iota(I32, (LANES, LANES), 0) < lax.broadcasted_iota(I32, (LANES, LANES), 1))
    running = jnp.dot(in_owner.astype(BF16), before.astype(F32).astype(BF16), preferred_element_type=F32)
    rank = jnp.sum(in_owner * running, axis=0, keepdims=True).astype(I32)
    slot = owner * SLOTS + rank
    place_t = (lax.broadcasted_iota(I32, (OWNERS * SLOTS, LANES), 0) == slot).astype(F32)
    pick = place_t.T.astype(BF16)
    for p in range(PAIRS):
        both = rows_ref[:, 16 * p: 16 * p + 16, :].astype(F32)
        for h in range(2):
            j = 2 * p + h
            block = both[:, 8 * h: 8 * h + 8, :].reshape(OWNERS * SLOTS, LANES).astype(BF16)
            cent_t = jnp.dot(pick, block, preferred_element_type=F32).T
            vec_t = vec_ref[:, 128 * j: 128 * j + 128].astype(F32).T
            resid_ref[128 * j: 128 * j + 128, :] = vec_t - cent_t
            stacked[16 * j: 16 * j + 16] = jnp.concatenate(
                [vec_t.reshape(16, WIDTH, LANES), cent_t.reshape(16, WIDTH, LANES)], axis=1).astype(BF16)

    level = lax.broadcasted_iota(I32, (CODES, LANES), 0)
    ones = jnp.ones((16, LANES), BF16)
    row8 = lax.broadcasted_iota(I32, (8, CODES), 0)

    def chunk(ch, _):
        count_tile = jnp.zeros((8, CODES), F32)
        for mm in range(CHUNK_SUBS):
            m = ch * CHUNK_SUBS + mm
            left = jnp.concatenate([stacked[m], ones], axis=0)
            for r in range(2):
                code = codes_ref[pl.ds(r * SUBS + m, 1), :]
                onehot = (level == code).astype(F32).astype(BF16)
                out = lax.dot_general(left, onehot, (((1,), (1,)), ((), ())), preferred_element_type=F32)
                sums_ref[ch, 16 * mm + 8 * r: 16 * mm + 8 * r + 8, :] = out[0:8] - out[8:16]
                count_tile = jnp.where(row8 == 2 * mm + r, out[16:24], count_tile)
        sums_ref[ch, 48:56, :] = count_tile
        return 0

    lax.fori_loop(0, CHUNKS, chunk, 0)


def local_totals(ids_row, rows, vectors, codes):
    return pl.pallas_call(
        totals_kernel,
        out_shape=(jax.ShapeDtypeStruct((CHUNKS, CHUNK_ROWS, CODES), F32),
                   jax.ShapeDtypeStruct((DIM, LANES), F32)),
        in_specs=[vmem()] * 4,
        out_specs=(vmem(), vmem()),
        scratch_shapes=[pltpu.VMEM((SUBS, 16, LANES), BF16)],
        compiler_params=pltpu.CompilerParams(vmem_limit_bytes=VMEM_LIMIT),
    )(ids_row, rows, vectors, codes)


def refit_kernel(sums_ref, book0_ref, book_ref, half, plane, line, plane_in, line_in,
                 core_send, core_recv, plane_send, plane_recv, line_send, line_recv,
                 unit_send, unit_recv, gather_send, gather_recv, back_send, back_recv):
    group, owner = place()
    x, core = group // 2, group % 2
    y, z = owner // 16, owner % 16
    xy = x * 4 + y
    sibling = group + 1 - 2 * core
    chunk = core * PLANE + xy

    def plane_device(i):
        return ((i // 4) * 2 + core, (i % 4) * 16 + z)

    barrier = pltpu.get_barrier_semaphore()
    pl.semaphore_signal(barrier, inc=1, device_id=(sibling, owner), device_id_type=MESH)
    for k in range(1, PLANE):
        pl.semaphore_signal(barrier, inc=1, device_id=plane_device((xy + k) % PLANE), device_id_type=MESH)
        pl.semaphore_signal(barrier, inc=1, device_id=(group, y * 16 + (z + k) % 16), device_id_type=MESH)
    pl.semaphore_wait(barrier, 1 + 2 * (PLANE - 1))

    def core_copy(k):
        i = (xy + 1 + k) % PLANE
        return pltpu.make_async_remote_copy(
            sums_ref.at[(1 - core) * PLANE + i], half.at[i], core_send.at[k], core_recv.at[k],
            device_id=(sibling, owner), device_id_type=MESH)

    def plane_copy(k):
        i = (xy + 1 + k) % PLANE
        return pltpu.make_async_remote_copy(
            plane.at[i], plane_in.at[xy], plane_send, plane_recv, device_id=plane_device(i), device_id_type=MESH)

    lax.fori_loop(0, PLANE, lambda k, _: (core_copy(k).start(), 0)[1], 0)

    def pass_on(k, _):
        i = (xy + 1 + k) % PLANE
        core_copy(k).wait_recv()
        plane[i] = sums_ref[core * PLANE + i] + half[i]

        @pl.when(k < PLANE - 1)
        def _():
            plane_copy(k).start()
        return 0

    lax.fori_loop(0, PLANE, pass_on, 0)
    plane_in[xy] = plane[xy]
    wait_bytes(plane.at[pl.ds(0, PLANE - 1)], plane_recv)
    for mm in range(CHUNK_SUBS):
        total = plane_in[0, 16 * mm: 16 * mm + 16, :]
        for i in range(1, PLANE):
            total = total + plane_in[i, 16 * mm: 16 * mm + 16, :]
        line[2 * mm, 0:16, :] = total[:, 0:128]
        line[2 * mm + 1, 0:16, :] = total[:, 128:256]
    total = plane_in[0, 48:56, :]
    for i in range(1, PLANE):
        total = total + plane_in[i, 48:56, :]
    for unit in range(6):
        side = unit % 2
        line[unit, 16:24, :] = total[:, 128 * side: 128 * side + 128]

    def line_copy(unit):
        return pltpu.make_async_remote_copy(
            line.at[unit], line_in.at[z], line_send.at[unit], line_recv,
            device_id=(group, y * 16 + UNIT_PLACES[unit]), device_id_type=MESH)

    for unit, where in enumerate(UNIT_PLACES):
        @pl.when(z != where)
        def _(unit=unit):
            line_copy(unit).start()

    def unit_ref(unit):
        mm, side = unit // 2, unit % 2
        return book_ref.at[chunk, 8 * mm: 8 * mm + 8, 128 * side: 128 * side + 128]

    def unit_copy(unit, k):
        return pltpu.make_async_remote_copy(
            unit_ref(unit), unit_ref(unit), unit_send, unit_recv.at[unit],
            device_id=(group, y * 16 + (z + k) % 16), device_id_type=MESH)

    for unit, where in enumerate(UNIT_PLACES):
        mm, side = unit // 2, unit % 2

        @pl.when(z == where)
        def _(unit=unit, mm=mm, side=side, where=where):
            line_in[where] = line[unit]
            wait_bytes(line_in.at[pl.ds(0, PLANE - 1)], line_recv)
            total = line_in[0]
            for i in range(1, PLANE):
                total = total + line_in[i]
            start = book0_ref[chunk, 8 * mm: 8 * mm + 8, 128 * side: 128 * side + 128]
            first = (total[0:8] + PRIOR * start) / (total[16 + 2 * mm: 17 + 2 * mm] + PRIOR)
            book_ref[chunk, 8 * mm: 8 * mm + 8, 128 * side: 128 * side + 128] = (
                (total[8:16] + PRIOR * first) / (total[17 + 2 * mm: 18 + 2 * mm] + PRIOR))
            lax.fori_loop(1, PLANE, lambda k, _: (unit_copy(unit, k).start(), 0)[1], 0)

    for unit, where in enumerate(UNIT_PLACES):
        @pl.when(z != where)
        def _(unit=unit):
            wait_bytes(unit_ref(unit), unit_recv.at[unit])

    def gather_copy(k):
        return pltpu.make_async_remote_copy(
            book_ref.at[chunk], book_ref.at[chunk], gather_send, gather_recv,
            device_id=plane_device((xy + k) % PLANE), device_id_type=MESH)

    lax.fori_loop(1, PLANE, lambda k, _: (gather_copy(k).start(), 0)[1], 0)
    wait_bytes(book_ref.at[pl.ds(0, PLANE - 1)], gather_recv)

    mine = book_ref.at[pl.ds(core * PLANE, PLANE)]
    back = pltpu.make_async_remote_copy(
        mine, mine, back_send, back_recv, device_id=(sibling, owner), device_id_type=MESH)
    back.start()

    lax.fori_loop(0, PLANE, lambda k, _: (core_copy(k).wait_send(), 0)[1], 0)
    wait_bytes(plane.at[pl.ds(0, PLANE - 1)], plane_send)
    for unit, where in enumerate(UNIT_PLACES):
        @pl.when(z != where)
        def _(unit=unit):
            line_copy(unit).wait_send()

        @pl.when(z == where)
        def _(unit=unit):
            def sent(k, _):
                unit_copy(unit, k).wait_send()
                return 0
            lax.fori_loop(1, PLANE, sent, 0)
    wait_bytes(book_ref.at[pl.ds(0, PLANE - 1)], gather_send)
    back.wait()


def refit(sums, book0):
    return pl.pallas_call(
        refit_kernel,
        out_shape=jax.ShapeDtypeStruct((CHUNKS, CHUNK_SUBS * WIDTH, CODES), F32),
        in_specs=[vmem()] * 2,
        out_specs=vmem(),
        scratch_shapes=[
            pltpu.VMEM((PLANE, CHUNK_ROWS, CODES), F32),
            pltpu.VMEM((PLANE, CHUNK_ROWS, CODES), F32),
            pltpu.VMEM((6, 24, LANES), F32),
            pltpu.VMEM((PLANE, CHUNK_ROWS, CODES), F32),
            pltpu.VMEM((PLANE, 24, LANES), F32),
            pltpu.SemaphoreType.DMA((PLANE,)), pltpu.SemaphoreType.DMA((PLANE,)),
            pltpu.SemaphoreType.DMA, pltpu.SemaphoreType.DMA,
            pltpu.SemaphoreType.DMA((6,)), pltpu.SemaphoreType.DMA,
            pltpu.SemaphoreType.DMA, pltpu.SemaphoreType.DMA((6,)),
            pltpu.SemaphoreType.DMA, pltpu.SemaphoreType.DMA,
            pltpu.SemaphoreType.DMA, pltpu.SemaphoreType.DMA,
        ],
        compiler_params=pltpu.CompilerParams(collective_id=1, has_side_effects=True, vmem_limit_bytes=VMEM_LIMIT),
    )(sums, book0)


def error_kernel(resid_ref, codes_ref, book_ref, key_ref, out_ref, mine, errors, parts, parts_in,
                 err_send, err_recv, part_send, part_recv):
    group, owner = place()
    barrier = pltpu.get_barrier_semaphore()

    def greet(k, _):
        pl.semaphore_signal(barrier, inc=1, device_id=(group, (owner + k) % OWNERS), device_id_type=MESH)
        return 0

    lax.fori_loop(1, OWNERS, greet, 0)
    for k in range(1, GROUPS):
        pl.semaphore_signal(barrier, inc=1, device_id=((group + k) % GROUPS, owner), device_id_type=MESH)

    def add(ch, total):
        for mm in range(CHUNK_SUBS):
            m = ch * CHUNK_SUBS + mm
            code = jnp.broadcast_to(codes_ref[pl.ds(SUBS + m, 1), :], (WIDTH, LANES))
            low = code & 127
            one = jnp.take_along_axis(book_ref[ch, 8 * mm: 8 * mm + 8, 0:128], low, axis=1)
            two = jnp.take_along_axis(book_ref[ch, 8 * mm: 8 * mm + 8, 128:256], low, axis=1)
            diff = resid_ref[pl.ds(8 * m, 8), :] - jnp.where(code > 127, two, one)
            total = total + diff * diff
        return total

    total = lax.fori_loop(0, CHUNKS, add, jnp.zeros((WIDTH, LANES), F32))
    mine[...] = jnp.sum(total, axis=0, keepdims=True) / float(DIM)
    pl.semaphore_wait(barrier, OWNERS - 1 + GROUPS - 1)

    def err_copy(k):
        return pltpu.make_async_remote_copy(
            mine, errors.at[owner], err_send, err_recv, device_id=(group, (owner + k) % OWNERS), device_id_type=MESH)

    lax.fori_loop(1, OWNERS, lambda k, _: (err_copy(k).start(), 0)[1], 0)
    errors[owner] = mine[...]
    wait_bytes(errors.at[pl.ds(0, OWNERS - 1)], err_recv)

    slot_base = lax.broadcasted_iota(I32, (OWNERS, SLOTS, LANES), 1).astype(F32) * 2048.0
    at = key_ref[...] - slot_base
    hit = (at > 0.5) & (at < 1024.5)
    which = jnp.sum(jnp.where(hit, at, 0.0), axis=2, keepdims=True).reshape(OWNERS * SLOTS, 1)
    value = jnp.sum(jnp.where(hit, jnp.broadcast_to(errors[...], hit.shape), 0.0), axis=2, keepdims=True)
    value = value.reshape(OWNERS * SLOTS, 1)
    lane = lax.broadcasted_iota(I32, (OWNERS * SLOTS, LANES), 1).astype(F32) + 1.0
    for block in range(GROUPS):
        chosen = jnp.where(which == lane + 128.0 * block, value, 0.0)
        parts[block] = jnp.sum(chosen, axis=0, keepdims=True)

    def part_copy(k):
        return pltpu.make_async_remote_copy(
            parts.at[(group + k) % GROUPS], parts_in.at[group], part_send, part_recv,
            device_id=((group + k) % GROUPS, owner), device_id_type=MESH)

    for k in range(1, GROUPS):
        part_copy(k).start()
    parts_in[group] = parts[group]
    wait_bytes(parts.at[pl.ds(0, GROUPS - 1)], part_recv)
    sum_here = parts_in[0]
    for i in range(1, GROUPS):
        sum_here = sum_here + parts_in[i]
    out_ref[...] = sum_here
    wait_bytes(parts.at[pl.ds(0, GROUPS - 1)], part_send)
    wait_bytes(errors.at[pl.ds(0, OWNERS - 1)], err_send)


def list_errors(resid, codes, book, key):
    return pl.pallas_call(
        error_kernel,
        out_shape=jax.ShapeDtypeStruct((1, LANES), F32),
        in_specs=[vmem()] * 4,
        out_specs=vmem(),
        scratch_shapes=[
            pltpu.VMEM((1, LANES), F32),
            pltpu.VMEM((OWNERS, 1, LANES), F32),
            pltpu.VMEM((GROUPS, 1, LANES), F32),
            pltpu.VMEM((GROUPS, 1, LANES), F32),
            pltpu.SemaphoreType.DMA, pltpu.SemaphoreType.DMA,
            pltpu.SemaphoreType.DMA, pltpu.SemaphoreType.DMA,
        ],
        compiler_params=pltpu.CompilerParams(collective_id=2, has_side_effects=True, vmem_limit_bytes=VMEM_LIMIT),
    )(resid, codes, book, key)


def local(vectors, list_ids, codes, centroids, codebook0):
    ids_row = list_ids.reshape(1, ROWS)
    rows, key = fetch_rows(ids_row, centroids)
    sums, resid = local_totals(ids_row, rows, vectors, codes)
    book = refit(sums, codebook0.reshape(CHUNKS, CHUNK_SUBS * WIDTH, CODES))
    list_error = list_errors(resid, codes, book, key)
    return book.reshape(SUBS, WIDTH, CODES), list_error.reshape(ROWS)


def solution(mesh):
    in_specs = (
        P(("groups", "owners"), None),
        P(("groups", "owners")),
        P(None, ("groups", "owners")),
        P(("groups", "owners"), None),
        P(),
    )
    out_specs = (P(), P(("groups", "owners")))
    return jax.shard_map(local, mesh=mesh, in_specs=in_specs, out_specs=out_specs, check_vma=False)
```

time: 786 us -> 153 us (0.19)
  waiting for transfers between devices: 538 us -> 0 us
  Pallas kernels: 0 us -> 146 us
  matrix products: 94.9 us -> 0 us
  local copies, waits for them, and re-layouts: 62.9 us -> 5.94 us
  starting transfers between devices: 33.6 us -> 0 us
  other arithmetic: 25.2 us -> 0 us
  between operations: 15 us -> 0.68 us
  blocking collectives: 12.3 us -> 0 us
    psum x1 -> x0, waiting for transfers between devices: 467 us -> none  [local(): lax.psum((code_sums, code_counts), ('groups', 'owners'))]
    pallas_call x0 -> x4, Pallas kernels: none -> 146 us  [the longest x1 69 us: fetch_rows(): pl.pallas_call(fetch_kernel, out_shape=(jax.ShapeDtypeStruct((OWNERS, 16...]
    dot_general x15 -> x0, matrix products: 94.9 us -> none  [the longest x6 38.6 us: add_block(): jnp.einsum('rmk,rmd->mkd', onehot, piece, precision=lax.Precision.HIGHEST)]
    all_to_all x3 -> x0, waiting for transfers between devices: 69.8 us -> none  [the longest x1 35 us: local(): lax.all_to_all(slot_rows, 'owners', split_axis=0, concat_axis=0, tiled=True)]
    all_to_all x3 -> x0, starting transfers between devices: 33.5 us -> none  [the longest x1 19.3 us: local(): lax.all_to_all(slot_list, 'owners', split_axis=0, concat_axis=0, tiled=True)]
    select_n x4 -> x0, other arithmetic: 17.6 us -> none  [the longest x1 17.6 us: local(): jnp.where(filled[:, None], got_rows.reshape(slot_total, feat_dim).astype(...]
    gather x2 -> x0, local copies, waits for them, and re-layouts: 16.2 us -> none  [local(): jnp.take(owned_rows, jnp.clip(held_flat_list, 0, list_total - 1), axis=0)]
    unnamed x16 -> x12, local copies, waits for them, and re-layouts: 19.6 us -> 5.94 us
  transfers between devices with their start and end apart: 5 -> 0, of which waited for: 4 -> 0; matrix products, arithmetic and copies ran while one was open for 3% -> 0% of each run, Pallas kernels for 0% -> 0%
where the time goes in v1:
time: 153 us; the launch traced here: 152 us
  Pallas kernels  146 us (95%)
  local copies, waits for them, and re-layouts  5.94 us (4%)
    pallas_call x1, Pallas kernels, fetch_rows(): pl.pallas_call(fetch_kernel, out_shape=(jax.ShapeDtypeStruct((OWNERS, 16...  69 us
    pallas_call x1, Pallas kernels, refit(): pl.pallas_call(refit_kernel, out_shape=jax.ShapeDtypeStruct((CHUNKS, CHUN...  48.6 us
    pallas_call x1, Pallas kernels, list_errors(): pl.pallas_call(error_kernel, out_shape=jax.ShapeDtypeStruct((1, LANES), F...  19.7 us
    pallas_call x1, Pallas kernels, local_totals(): pl.pallas_call(totals_kernel, out_shape=(jax.ShapeDtypeStruct((CHUNKS, CH...  8.43 us
    unnamed x12, local copies, waits for them, and re-layouts  5.94 us

profile of v1, /device:TPU:1, one launch (start us, length us, event | category | flops | bytes accessed | tf_op | source)
XLA Modules:
  0.0 152.3 jit_solution(8784888025160188432)
XLA Ops:
  0.6 0.0 copy-start.2
  0.6 0.9 copy-done.2
  1.6 0.0 copy-start.4
  1.6 0.7 copy-done.4
  2.2 69.0 %shard_map.68 = (bf16[64,48,128]{2,1,0:T(8,128)(2,1)S(1)}, f32[64,1,128]{2,1,0:T(1,128)S(1)}) custom-call(s32[1,128]{1,0:T(1,128)S(1)} %bitcast.6, bf16[128,768]{1,0:T(8,128)(2,1)S(1)} %copy-done.2), custom_call_target="tpu_custom_call" | custom-call | tf_op jit(solution)/shard_map/pallas_call | solution.py:148
  71.2 0.0 copy-start.1
  71.2 0.9 copy-done.1
  72.1 0.0 copy-start.3
  72.1 0.9 copy-done.3
  73.0 8.4 %shard_map.69 = (f32[32,56,256]{2,1,0:T(8,128)S(1)}, f32[768,128]{1,0:T(8,128)S(1)}) custom-call(s32[1,128]{1,0:T(1,128)S(1)} %bitcast.7, bf16[64,48,128]{2,1,0:T(8,128)(2,1)S(1)} %get-tuple-element.6.rows_ref, bf16[128,768]{1,0:T(8,128)(2,1)S(1)} %copy-done.3, s32[192,128]{1,0:T(8,128)S(1)} %copy-done.1), custom_call_target="tpu_custom_call" | custom-call | tf_op jit(solution)/shard_map/pallas_call | solution.py:210
  81.5 0.0 copy-start
  81.5 1.2 copy-done
  82.6 48.6 %shard_map.70.book_ref = f32[32,24,256]{2,1,0:T(8,128)S(1)} custom-call(f32[32,56,256]{2,1,0:T(8,128)S(1)} %get-tuple-element.7.sums_ref, f32[32,24,256]{2,1,0:T(8,128)S(1)} %bitcast.5), custom_call_target="tpu_custom_call" | custom-call | tf_op jit(solution)/shard_map/pallas_call | solution.py:351
  131.3 19.7 %shard_map.71 = f32[1,128]{1,0:T(1,128)S(1)} custom-call(f32[768,128]{1,0:T(8,128)S(1)} %get-tuple-element.8.resid_ref, s32[192,128]{1,0:T(8,128)S(1)} %copy-done.1, f32[32,24,256]{2,1,0:T(8,128)S(1)} %shard_map.70.book_ref, f32[64,1,128]{2,1,0:T(1,128)S(1)} %get-tuple-element.9.key_ref), custom_call_target="tpu_custom_call" | custom-call | tf_op jit(solution)/shard_map/pallas_call | solution.py:438
  151.0 0.9 copy.9
  151.8 0.5 copy.10
Async XLA Ops:
  0.6 0.9 copy-start.2
  1.6 0.7 copy-start.4
  71.2 0.9 copy-start.1
  72.1 0.9 copy-start.3
  81.5 1.2 copy-start

commit v2 on v0

v2 whole, which is shorter than its diff:
```python
import jax
import jax.numpy as jnp
from jax import lax
from jax.experimental import pallas as pl
from jax.experimental.pallas import tpu as pltpu
from jax.sharding import PartitionSpec as P

MESH = pl.DeviceIdType.MESH
F32 = jnp.float32
BF16 = jnp.bfloat16
I32 = jnp.int32

ROWS = 128
DIM = 768
SUBS = 96
WIDTH = 8
CODES = 256
OWNERS = 64
GROUPS = 8
CAP = 6
SLOTS = 8
LANES = 128
PAIRS = 3
LISTS_HERE = GROUPS * ROWS
CHUNKS = 32
CHUNK_SUBS = SUBS // CHUNKS
CHUNK_ROWS = 56
PLANE = 16
PRIOR = 128.0
UNIT_PLACES = (0, 2, 5, 8, 10, 13)
HELD = CAP * OWNERS
VMEM_LIMIT = 48 * 1024 * 1024


def vmem():
    return pl.BlockSpec(memory_space=pltpu.VMEM)


def wait_bytes(ref, sem):
    pltpu.make_async_copy(ref, ref, sem).wait()


def place():
    group, owner = lax.axis_index("groups"), lax.axis_index("owners")
    return group, owner


def local_copy(src, dst, sem):
    copy = pltpu.make_async_copy(src, dst, sem)
    copy.start()
    return copy


def each(first, last, body):
    def step(k, carry):
        body(k)
        return carry
    lax.fori_loop(first, last, step, 0)


def index_kernel(ids_hbm, vec_hbm, codes_hbm, cent_hbm, book0_hbm, book_ref, out_ref,
                 ids_v, vec_v, codes_v, book0_v, table, place_v, vec_t, vec_out, vec_in, code_out, code_in,
                 code_f, held_codes, pick_v, base_t, sums, half, plane, plane_in, line, line_in, parts, parts_in,
                 load_sem, code_send, code_recv, vec_send, vec_recv, x_send, x_recv, sib_send, sib_recv,
                 core_send, core_recv, plane_send, plane_recv, line_send, line_recv,
                 unit_send, unit_recv, gather_send, gather_recv, back_send, back_recv, part_send, part_recv):
    group, owner = place()
    x, core = group // 2, group % 2
    y, z = owner // 16, owner % 16
    xy = x * 4 + y
    sibling = group + 1 - 2 * core
    chunk = core * PLANE + xy

    def plane_device(i):
        return ((i // 4) * 2 + core, (i % 4) * 16 + z)

    barrier = pltpu.get_barrier_semaphore()
    each(1, OWNERS, lambda k: pl.semaphore_signal(
        barrier, inc=1, device_id=(group, (owner + k) % OWNERS), device_id_type=MESH))
    for k in range(1, GROUPS):
        pl.semaphore_signal(barrier, inc=1, device_id=((group + k) % GROUPS, owner), device_id_type=MESH)
    for i in range(1, 4):
        for j in range(1, 4):
            pl.semaphore_signal(
                barrier, inc=1, device_id=((group + 2 * i) % GROUPS, (owner + 16 * j) % OWNERS), device_id_type=MESH)

    load_ids = local_copy(ids_hbm, ids_v, load_sem.at[0])
    load_codes = local_copy(codes_hbm, codes_v, load_sem.at[1])
    load_vec = local_copy(vec_hbm, vec_v, load_sem.at[2])
    load_cent = local_copy(cent_hbm, table.at[group], load_sem.at[3])
    load_book = local_copy(book0_hbm.at[chunk], book0_v, load_sem.at[4])

    load_ids.wait()
    ids = ids_v[...]
    owner_of = (ids >> 7) & (OWNERS - 1)
    in_owner = (lax.broadcasted_iota(I32, (OWNERS, LANES), 0) == owner_of).astype(F32)
    before = (lax.broadcasted_iota(I32, (LANES, LANES), 0) < lax.broadcasted_iota(I32, (LANES, LANES), 1))
    running = jnp.dot(in_owner.astype(BF16), before.astype(F32).astype(BF16), preferred_element_type=F32)
    rank = jnp.sum(in_owner * running, axis=0, keepdims=True).astype(I32)
    slot = owner_of * SLOTS + rank
    place_v[...] = (lax.broadcasted_iota(I32, (OWNERS * SLOTS, LANES), 0) == slot).astype(F32).astype(BF16)
    list_no = ((ids >> 13) << 7) + (ids & 127) + 1

    def pack(rows):
        both = jnp.concatenate([rows[:, 0:128].reshape(OWNERS, SLOTS, LANES),
                                rows[:, 128:256].reshape(OWNERS, SLOTS, LANES)], axis=1)
        return both.astype(BF16)

    load_codes.wait()
    row8 = lax.broadcasted_iota(I32, (8, LANES), 0)
    list_rows = jnp.where(row8 == 0, list_no >> 8, jnp.where(row8 == 1, list_no & 255, 0)).astype(F32)
    load = jnp.concatenate(
        [codes_v[...].astype(F32), list_rows, jnp.zeros((CODES - 2 * SUBS - 8, LANES), F32)], axis=0).astype(BF16)
    code_out[...] = pack(lax.dot_general(
        place_v[...], load, (((1,), (1,)), ((), ())), preferred_element_type=F32))

    load_cent.wait()
    pl.semaphore_wait(barrier, OWNERS - 1 + GROUPS - 1 + 9)

    def code_copy(k):
        peer = (owner + k) % OWNERS
        return pltpu.make_async_remote_copy(
            code_out.at[peer], code_in.at[owner], code_send, code_recv, device_id=(group, peer), device_id_type=MESH)

    def vec_copy(k):
        peer = (owner + k) % OWNERS
        return pltpu.make_async_remote_copy(
            vec_out.at[peer], vec_in.at[owner], vec_send, vec_recv, device_id=(group, peer), device_id_type=MESH)

    across = []
    for j in range(1, 4):
        across.append(pltpu.make_async_remote_copy(
            table.at[group], table.at[group], x_send.at[j - 1], x_recv.at[j - 1],
            device_id=((group + 2 * j) % GROUPS, owner), device_id_type=MESH))
    aside = [pltpu.make_async_remote_copy(
        table.at[group], table.at[group], sib_send.at[0], sib_recv.at[0],
        device_id=(sibling, owner), device_id_type=MESH)]
    each(1, OWNERS, lambda k: code_copy(k).start())
    for copy in across + aside:
        copy.start()
    code_in[owner] = code_out[owner]

    load_vec.wait()
    for p in range(PAIRS):
        rows = jnp.dot(place_v[...], vec_v[:, 256 * p: 256 * p + 256], preferred_element_type=F32)
        vec_out[:, 16 * p: 16 * p + 16, :] = pack(rows)
        for h in range(2):
            j = 2 * p + h
            vec_t[128 * j: 128 * j + 128, :] = vec_v[:, 128 * j: 128 * j + 128].astype(F32).T
    vec_in[owner] = vec_out[owner]

    for j in range(1, 4):
        source = (group + 2 * GROUPS - 2 * j) % GROUPS
        across[j - 1].wait_recv()
        relay = pltpu.make_async_remote_copy(
            table.at[source], table.at[source], sib_send.at[j], sib_recv.at[j],
            device_id=(sibling, owner), device_id_type=MESH)
        relay.start()
        aside.append(relay)

    ones = jnp.ones((8, LANES), F32)
    tile_row = lax.broadcasted_iota(I32, (8, CODES), 0)
    level = lax.broadcasted_iota(I32, (CODES, LANES), 0)

    def vector_sums(ch):
        count_tile = jnp.zeros((8, CODES), F32)
        for mm in range(CHUNK_SUBS):
            m = ch * CHUNK_SUBS + mm
            left = jnp.concatenate([vec_t[pl.ds(8 * m, 8), :], ones], axis=0).astype(BF16)
            for r in range(2):
                onehot = (level == codes_v[pl.ds(r * SUBS + m, 1), :]).astype(F32).astype(BF16)
                out = lax.dot_general(left, onehot, (((1,), (1,)), ((), ())), preferred_element_type=F32)
                sums[ch, 16 * mm + 8 * r: 16 * mm + 8 * r + 8, :] = out[0:8]
                count_tile = jnp.where(tile_row == 2 * mm + r, out[8:16], count_tile)
        sums[ch, 48:56, :] = count_tile

    each(0, CHUNKS, vector_sums)

    wait_bytes(code_in.at[pl.ds(0, OWNERS - 1)], code_recv)
    each(1, OWNERS, lambda k: vec_copy(k).start())

    code_f[...] = code_in[...].astype(F32)
    for h in range(2):
        rows = jnp.concatenate([code_f[:, 8 * h + s, :] for s in range(CAP)], axis=0)
        held_codes[128 * h: 128 * h + 128, :] = rows.T.astype(I32)
        if h == 1:
            which = rows[:, 64:65] * 256.0 + rows[:, 65:66]
    lane = lax.broadcasted_iota(I32, (HELD, LISTS_HERE), 1).astype(F32) + 1.0
    pick_v[...] = (which == lane).astype(F32).astype(BF16)
    for copy in aside:
        copy.wait_recv()
    for j in range(6):
        lists = table[:, :, 128 * j: 128 * j + 128].reshape(LISTS_HERE, LANES)
        base_t[128 * j: 128 * j + 128, :] = jnp.dot(pick_v[...], lists, preferred_element_type=F32).T

    wide = lax.broadcasted_iota(I32, (CODES, HELD), 0)

    def centroid_sums(ch):
        for mm in range(CHUNK_SUBS):
            m = ch * CHUNK_SUBS + mm
            left = base_t[pl.ds(8 * m, 8), :].astype(BF16)
            for r in range(2):
                onehot = (wide == held_codes[pl.ds(r * SUBS + m, 1), :]).astype(F32).astype(BF16)
                out = lax.dot_general(left, onehot, (((1,), (1,)), ((), ())), preferred_element_type=F32)
                sums[ch, 16 * mm + 8 * r: 16 * mm + 8 * r + 8, :] -= out

    def core_copy(k):
        i = (xy + 1 + k) % PLANE
        return pltpu.make_async_remote_copy(
            sums.at[(1 - core) * PLANE + i], half.at[i], core_send.at[k], core_recv.at[k],
            device_id=(sibling, owner), device_id_type=MESH)

    def plane_copy(k):
        i = (xy + 1 + k) % PLANE
        return pltpu.make_async_remote_copy(
            plane.at[i], plane_in.at[xy], plane_send, plane_recv, device_id=plane_device(i), device_id_type=MESH)

    def other_half(k):
        centroid_sums((1 - core) * PLANE + (xy + 1 + k) % PLANE)
        core_copy(k).start()

    each(0, PLANE, other_half)

    def own_half(k):
        i = (xy + 1 + k) % PLANE
        centroid_sums(core * PLANE + i)
        core_copy(k).wait_recv()
        plane[i] = sums[core * PLANE + i] + half[i]

        @pl.when(k < PLANE - 1)
        def _():
            plane_copy(k).start()

    each(0, PLANE, own_half)
    plane_in[xy] = plane[xy]
    wait_bytes(plane.at[pl.ds(0, PLANE - 1)], plane_recv)
    for mm in range(CHUNK_SUBS):
        total = plane_in[0, 16 * mm: 16 * mm + 16, :]
        for i in range(1, PLANE):
            total = total + plane_in[i, 16 * mm: 16 * mm + 16, :]
        line[2 * mm, 0:16, :] = total[:, 0:128]
        line[2 * mm + 1, 0:16, :] = total[:, 128:256]
    total = plane_in[0, 48:56, :]
    for i in range(1, PLANE):
        total = total + plane_in[i, 48:56, :]
    for unit in range(6):
        side = unit % 2
        line[unit, 16:24, :] = total[:, 128 * side: 128 * side + 128]

    def line_copy(unit):
        return pltpu.make_async_remote_copy(
            line.at[unit], line_in.at[z], line_send.at[unit], line_recv,
            device_id=(group, y * 16 + UNIT_PLACES[unit]), device_id_type=MESH)

    for unit, where in enumerate(UNIT_PLACES):
        @pl.when(z != where)
        def _(unit=unit):
            line_copy(unit).start()

    def unit_ref(unit):
        mm, side = unit // 2, unit % 2
        return book_ref.at[chunk, 8 * mm: 8 * mm + 8, 128 * side: 128 * side + 128]

    def unit_copy(unit, k):
        return pltpu.make_async_remote_copy(
            unit_ref(unit), unit_ref(unit), unit_send, unit_recv.at[unit],
            device_id=(group, y * 16 + (z + k) % 16), device_id_type=MESH)

    load_book.wait()
    for unit, where in enumerate(UNIT_PLACES):
        mm, side = unit // 2, unit % 2

        @pl.when(z == where)
        def _(unit=unit, mm=mm, side=side, where=where):
            line_in[where] = line[unit]
            wait_bytes(line_in.at[pl.ds(0, PLANE - 1)], line_recv)
            total = line_in[0]
            for i in range(1, PLANE):
                total = total + line_in[i]
            start = book0_v[8 * mm: 8 * mm + 8, 128 * side: 128 * side + 128]
            first = (total[0:8] + PRIOR * start) / (total[16 + 2 * mm: 17 + 2 * mm] + PRIOR)
            book_ref[chunk, 8 * mm: 8 * mm + 8, 128 * side: 128 * side + 128] = (
                (total[8:16] + PRIOR * first) / (total[17 + 2 * mm: 18 + 2 * mm] + PRIOR))
            each(1, PLANE, lambda k: unit_copy(unit, k).start())

    wait_bytes(vec_in.at[pl.ds(0, OWNERS - 1)], vec_recv)
    for p in range(PAIRS):
        code_f[...] = vec_in[:, 16 * p: 16 * p + 16, :].astype(F32)
        for h in range(2):
            j = 2 * p + h
            rows = jnp.concatenate([code_f[:, 8 * h + s, :] for s in range(CAP)], axis=0)
            base_t[128 * j: 128 * j + 128, :] = rows.T - base_t[128 * j: 128 * j + 128, :]

    for unit, where in enumerate(UNIT_PLACES):
        @pl.when(z != where)
        def _(unit=unit):
            wait_bytes(unit_ref(unit), unit_recv.at[unit])

    def gather_copy(k):
        return pltpu.make_async_remote_copy(
            book_ref.at[chunk], book_ref.at[chunk], gather_send, gather_recv,
            device_id=plane_device((xy + k) % PLANE), device_id_type=MESH)

    each(1, PLANE, lambda k: gather_copy(k).start())
    wait_bytes(book_ref.at[pl.ds(0, PLANE - 1)], gather_recv)

    mine = book_ref.at[pl.ds(core * PLANE, PLANE)]
    back = pltpu.make_async_remote_copy(
        mine, mine, back_send, back_recv, device_id=(sibling, owner), device_id_type=MESH)
    back.start()

    def add(ch, totals):
        for mm in range(CHUNK_SUBS):
            m = ch * CHUNK_SUBS + mm
            left = book_ref[ch, 8 * mm: 8 * mm + 8, 0:128]
            right = book_ref[ch, 8 * mm: 8 * mm + 8, 128:256]
            row = jnp.broadcast_to(held_codes[pl.ds(SUBS + m, 1), :], (WIDTH, HELD))
            new = []
            for t in range(HELD // LANES):
                code = row[:, 128 * t: 128 * t + 128]
                low = code & 127
                one = jnp.take_along_axis(left, low, axis=1)
                two = jnp.take_along_axis(right, low, axis=1)
                diff = base_t[pl.ds(8 * m, 8), 128 * t: 128 * t + 128] - jnp.where(code > 127, two, one)
                new.append(totals[t] + diff * diff)
            totals = tuple(new)
        return totals

    zero = jnp.zeros((WIDTH, LANES), F32)
    totals = lax.fori_loop(core * PLANE, core * PLANE + PLANE, add, (zero,) * 3)
    back.wait_recv()
    totals = lax.fori_loop((1 - core) * PLANE, (1 - core) * PLANE + PLANE, add, totals)
    error = jnp.concatenate([jnp.sum(t, axis=0, keepdims=True) for t in totals], axis=1) / float(DIM)
    top = error.astype(BF16).astype(F32)
    mid = (error - top).astype(BF16).astype(F32)
    low = error - top - mid
    row = lax.broadcasted_iota(I32, (16, HELD), 0)
    split = jnp.where(row == 0, top, jnp.where(row == 1, mid, jnp.where(row == 2, low, 0.0))).astype(BF16)
    by_list = jnp.sum(jnp.dot(split, pick_v[...], preferred_element_type=F32), axis=0, keepdims=True)
    for i in range(GROUPS):
        parts[i] = by_list[:, 128 * i: 128 * i + 128]

    def part_copy(k):
        return pltpu.make_async_remote_copy(
            parts.at[(group + k) % GROUPS], parts_in.at[group], part_send, part_recv,
            device_id=((group + k) % GROUPS, owner), device_id_type=MESH)

    for k in range(1, GROUPS):
        part_copy(k).start()
    parts_in[group] = parts[group]

    wait_bytes(code_in.at[pl.ds(0, OWNERS - 1)], code_send)
    wait_bytes(vec_in.at[pl.ds(0, OWNERS - 1)], vec_send)
    for copy in across + aside:
        copy.wait_send()
    each(0, PLANE, lambda k: core_copy(k).wait_send())
    wait_bytes(plane.at[pl.ds(0, PLANE - 1)], plane_send)
    for unit, where in enumerate(UNIT_PLACES):
        @pl.when(z != where)
        def _(unit=unit):
            line_copy(unit).wait_send()

        @pl.when(z == where)
        def _(unit=unit):
            each(1, PLANE, lambda k: unit_copy(unit, k).wait_send())
    wait_bytes(book_ref.at[pl.ds(0, PLANE - 1)], gather_send)
    back.wait_send()

    wait_bytes(parts.at[pl.ds(0, GROUPS - 1)], part_recv)
    sum_here = parts_in[0]
    for i in range(1, GROUPS):
        sum_here = sum_here + parts_in[i]
    out_ref[...] = sum_here
    wait_bytes(parts.at[pl.ds(0, GROUPS - 1)], part_send)


def local(vectors, list_ids, codes, centroids, codebook0):
    dma = pltpu.SemaphoreType.DMA
    any_place = pl.BlockSpec(memory_space=pl.ANY)
    book, list_error = pl.pallas_call(
        index_kernel,
        out_shape=(jax.ShapeDtypeStruct((CHUNKS, CHUNK_SUBS * WIDTH, CODES), F32),
                   jax.ShapeDtypeStruct((1, LANES), F32)),
        in_specs=[any_place] * 5,
        out_specs=(vmem(), vmem()),
        scratch_shapes=[
            pltpu.VMEM((1, LANES), I32),
            pltpu.VMEM((ROWS, DIM), BF16),
            pltpu.VMEM((2 * SUBS, LANES), I32),
            pltpu.VMEM((CHUNK_SUBS * WIDTH, CODES), F32),
            pltpu.VMEM((GROUPS, ROWS, DIM), BF16),
            pltpu.VMEM((OWNERS * SLOTS, LANES), BF16),
            pltpu.VMEM((DIM, LANES), F32),
            pltpu.VMEM((OWNERS, 16 * PAIRS, LANES), BF16),
            pltpu.VMEM((OWNERS, 16 * PAIRS, LANES), BF16),
            pltpu.VMEM((OWNERS, 16, LANES), BF16),
            pltpu.VMEM((OWNERS, 16, LANES), BF16),
            pltpu.VMEM((OWNERS, 16, LANES), F32),
            pltpu.VMEM((CODES, HELD), I32),
            pltpu.VMEM((HELD, LISTS_HERE), BF16),
            pltpu.VMEM((DIM, HELD), F32),
            pltpu.VMEM((CHUNKS, CHUNK_ROWS, CODES), F32),
            pltpu.VMEM((PLANE, CHUNK_ROWS, CODES), F32),
            pltpu.VMEM((PLANE, CHUNK_ROWS, CODES), F32),
            pltpu.VMEM((PLANE, CHUNK_ROWS, CODES), F32),
            pltpu.VMEM((6, 24, LANES), F32),
            pltpu.VMEM((PLANE, 24, LANES), F32),
            pltpu.VMEM((GROUPS, 1, LANES), F32),
            pltpu.VMEM((GROUPS, 1, LANES), F32),
            dma((5,)),
            dma, dma, dma, dma,
            dma((3,)), dma((3,)), dma((4,)), dma((4,)),
            dma((PLANE,)), dma((PLANE,)),
            dma, dma,
            dma((6,)), dma,
            dma, dma((6,)),
            dma, dma, dma, dma, dma, dma,
        ],
        compiler_params=pltpu.CompilerParams(collective_id=0, has_side_effects=True, vmem_limit_bytes=VMEM_LIMIT),
    )(list_ids.reshape(1, ROWS), vectors, codes, centroids,
      codebook0.reshape(CHUNKS, CHUNK_SUBS * WIDTH, CODES))
    return book.reshape(SUBS, WIDTH, CODES), list_error.reshape(ROWS)


def solution(mesh):
    in_specs = (
        P(("groups", "owners"), None),
        P(("groups", "owners")),
        P(None, ("groups", "owners")),
        P(("groups", "owners"), None),
        P(),
    )
    out_specs = (P(), P(("groups", "owners")))
    return jax.shard_map(local, mesh=mesh, in_specs=in_specs, out_specs=out_specs, check_vma=False)
```

time: 786 us -> 105 us (0.13)
  waiting for transfers between devices: 538 us -> 0 us
  Pallas kernels: 0 us -> 98.7 us
  matrix products: 94.9 us -> 0 us
  local copies, waits for them, and re-layouts: 62.9 us -> 5.92 us
  starting transfers between devices: 33.6 us -> 0 us
  other arithmetic: 25.2 us -> 0 us
  between operations: 15 us -> 0.65 us
  blocking collectives: 12.3 us -> 0 us
    psum x1 -> x0, waiting for transfers between devices: 467 us -> none  [local(): lax.psum((code_sums, code_counts), ('groups', 'owners'))]
    pallas_call x0 -> x1, Pallas kernels: none -> 98.7 us  [local(): pl.pallas_call(index_kernel, out_shape=(jax.ShapeDtypeStruct((CHUNKS, CHU...]
    dot_general x15 -> x0, matrix products: 94.9 us -> none  [the longest x6 38.6 us: add_block(): jnp.einsum('rmk,rmd->mkd', onehot, piece, precision=lax.Precision.HIGHEST)]
    all_to_all x3 -> x0, waiting for transfers between devices: 69.8 us -> none  [the longest x1 35 us: local(): lax.all_to_all(slot_rows, 'owners', split_axis=0, concat_axis=0, tiled=True)]
    all_to_all x3 -> x0, starting transfers between devices: 33.5 us -> none  [the longest x1 19.3 us: local(): lax.all_to_all(slot_list, 'owners', split_axis=0, concat_axis=0, tiled=True)]
    select_n x4 -> x0, other arithmetic: 17.6 us -> none  [the longest x1 17.6 us: local(): jnp.where(filled[:, None], got_rows.reshape(slot_total, feat_dim).astype(...]
    gather x2 -> x0, local copies, waits for them, and re-layouts: 16.2 us -> none  [local(): jnp.take(owned_rows, jnp.clip(held_flat_list, 0, list_total - 1), axis=0)]
    unnamed x16 -> x12, local copies, waits for them, and re-layouts: 19.6 us -> 5.92 us
  transfers between devices with their start and end apart: 5 -> 0, of which waited for: 4 -> 0; matrix products, arithmetic and copies ran while one was open for 3% -> 0% of each run, Pallas kernels for 0% -> 0%
where the time goes in v2:
time: 105 us
  Pallas kernels  98.7 us (94%)
  local copies, waits for them, and re-layouts  5.92 us (6%)
    pallas_call x1, Pallas kernels, local(): pl.pallas_call(index_kernel, out_shape=(jax.ShapeDtypeStruct((CHUNKS, CHU...  98.7 us
    unnamed x12, local copies, waits for them, and re-layouts  5.92 us

profile of v2, /device:TPU:1, one launch (start us, length us, event | category | flops | bytes accessed | tf_op | source)
XLA Modules:
  0.0 105.2 jit_solution(15922291145787738582)
XLA Ops:
  0.6 0.0 copy-start.4
  0.6 0.6 copy-done.4
  1.3 0.0 copy-start
  1.3 1.1 %copy-done = f32[96,8,256]{2,1,0:T(8,128)S(1)} copy-done((f32[96,8,256]{2,1,0:T(8,128)S(1)}, f32[96,8,256]{2,1,0:T(8,128)}, u32[]{:S(2)}) %copy-start) | copy-done | bytes 786456
  2.4 0.0 copy-start.1
  2.4 0.9 copy-done.1
  3.3 0.0 copy-start.2
  3.4 0.9 copy-done.2
  4.3 0.0 copy-start.3
  4.3 0.9 copy-done.3
  5.2 98.7 %shard_map.68 = (f32[32,24,256]{2,1,0:T(8,128)S(1)}, f32[1,128]{1,0:T(1,128)S(1)}) custom-call(s32[1,128]{1,0:T(1,128)S(1)} %bitcast.6, bf16[128,768]{1,0:T(8,128)(2,1)S(1)} %copy-done.1, s32[192,128]{1,0:T(8,128)S(1)} %copy-done.3, bf16[128,768]{1,0:T(8,128)(2,1)S(1)} %copy-done.2, f32[32,24,256]{2,1,0:T(8,128)S(1)} %bitcast.4), custom_call_target="tpu_custom_call" | custom-call | tf_op jit(solution)/shard_map/pallas_call | solution.py:380
  103.8 0.9 copy.9
  104.7 0.5 copy.10
Async XLA Ops:
  0.6 0.7 copy-start.4
  1.3 1.1 %copy-start = (f32[96,8,256]{2,1,0:T(8,128)S(1)}, f32[96,8,256]{2,1,0:T(8,128)}, u32[]{:S(2)}) copy-start(f32[96,8,256]{2,1,0:T(8,128)} %param.9) | copy-start | bytes 2359300
  2.4 0.9 copy-start.1
  3.3 0.9 copy-start.2
  4.3 0.9 copy-start.3

commit v3 on v2

v3 whole, which is shorter than its diff:
```python
import jax
import jax.numpy as jnp
from jax import lax
from jax.experimental import pallas as pl
from jax.experimental.pallas import tpu as pltpu
from jax.sharding import PartitionSpec as P

MESH = pl.DeviceIdType.MESH
F32 = jnp.float32
BF16 = jnp.bfloat16
I32 = jnp.int32

ROWS = 128
DIM = 768
SUBS = 96
WIDTH = 8
CODES = 256
OWNERS = 64
GROUPS = 8
CAP = 6
SLOTS = 8
LANES = 128
PAIRS = 2
LISTS_HERE = GROUPS * ROWS
CHUNKS = 32
CHUNK_SUBS = SUBS // CHUNKS
CHUNK_ROWS = 2 * CHUNK_SUBS * WIDTH
PLANE = 16
PRIOR = 128.0
UNIT_PLACES = (0, 2, 5, 8, 10, 13)
VEC_FIRST = 28
HELD = CAP * OWNERS
VMEM_LIMIT = 60 * 1024 * 1024


def vmem():
    return pl.BlockSpec(memory_space=pltpu.VMEM)


def wait_bytes(ref, sem):
    pltpu.make_async_copy(ref, ref, sem).wait()


def place():
    group, owner = lax.axis_index("groups"), lax.axis_index("owners")
    return group, owner


def local_copy(src, dst, sem):
    copy = pltpu.make_async_copy(src, dst, sem)
    copy.start()
    return copy


def each(first, last, body):
    def step(k, carry):
        body(k)
        return carry
    lax.fori_loop(first, last, step, 0)


def index_kernel(ids_hbm, vec_hbm, codes_hbm, cent_hbm, book0_hbm, book_ref, out_ref,
                 ids_v, vec_v, codes_v, book0_v, table, place_v, spare_v, vec_t, vec_out, vec_in, code_out, code_in,
                 code_f, spare_f, held_codes, pick_v, base_t, sums, half, plane, plane_in, line, line_in, parts, parts_in,
                 tally, tally_half, tally_plane, tally_plane_in, tally_line, tally_line_in,
                 load_sem, code_send, code_recv, vec_send, vec_recv, x_send, x_recv, sib_send, sib_recv,
                 core_send, core_recv, plane_send, plane_recv, line_send, line_recv,
                 unit_send, unit_recv, gather_send, gather_recv, back_send, back_recv, part_send, part_recv,
                 t_core_send, t_core_recv, t_plane_send, t_plane_recv, t_line_send, t_line_recv):
    group, owner = place()
    x, core = group // 2, group % 2
    y, z = owner // 16, owner % 16
    xy = x * 4 + y
    sibling = group + 1 - 2 * core
    chunk = core * PLANE + xy

    def plane_device(i):
        return ((i // 4) * 2 + core, (i % 4) * 16 + z)

    def plane_to(k):
        step = (7 * k) % PLANE
        return (x + step // 4) % 4 * 4 + (y + step % 4) % 4

    def plane_from(k):
        step = (7 * k) % PLANE
        return (x + 4 - step // 4) % 4 * 4 + (y + 4 - step % 4) % 4

    def far_first(j):
        return (8 + (1 - 2 * (j % 2)) * ((j + 1) // 2)) % 16

    load_ids = local_copy(ids_hbm, ids_v, load_sem.at[0])
    load_codes = local_copy(codes_hbm, codes_v, load_sem.at[1])
    load_vec = local_copy(vec_hbm, vec_v, load_sem.at[2])
    load_cent = local_copy(cent_hbm, table.at[group], load_sem.at[3])
    load_book = local_copy(book0_hbm.at[chunk], book0_v, load_sem.at[4])

    barrier = pltpu.get_barrier_semaphore()

    def nth_peer(k):
        return (y + 3 - k % 4) % 4 * 16 + (z + far_first(k // 4)) % 16

    each(0, OWNERS - 1, lambda k: pl.semaphore_signal(
        barrier, inc=1, device_id=(group, nth_peer(k)), device_id_type=MESH))
    for k in range(1, GROUPS):
        pl.semaphore_signal(barrier, inc=1, device_id=((group + k) % GROUPS, owner), device_id_type=MESH)
    for i in range(1, 4):
        for j in range(1, 4):
            pl.semaphore_signal(
                barrier, inc=1, device_id=((group + 2 * i) % GROUPS, (owner + 16 * j) % OWNERS), device_id_type=MESH)

    load_ids.wait()
    ids = ids_v[...]
    owner_of = (ids >> 7) & (OWNERS - 1)
    in_owner = (lax.broadcasted_iota(I32, (OWNERS, LANES), 0) == owner_of).astype(F32)
    before = (lax.broadcasted_iota(I32, (LANES, LANES), 0) < lax.broadcasted_iota(I32, (LANES, LANES), 1))
    running = jnp.dot(in_owner.astype(BF16), before.astype(F32).astype(BF16), preferred_element_type=F32)
    rank = jnp.sum(in_owner * running, axis=0, keepdims=True).astype(I32)
    slot = owner_of * SLOTS + rank
    place_v[...] = (lax.broadcasted_iota(I32, (OWNERS * SLOTS, LANES), 0) == slot).astype(F32).astype(BF16)
    for q in range(3):
        here = jnp.where((rank >> 1) == q, slot + 6 - 2 * q, -1)
        spare_v[q] = (lax.broadcasted_iota(I32, (OWNERS * SLOTS, LANES), 0) == here).astype(F32).astype(BF16)
    list_no = ((ids >> 13) << 7) + (ids & 127) + 1

    def extra(part):
        block = 4 + part // 3
        return jnp.dot(spare_v[part % 3], vec_v[:, 128 * block: 128 * block + 128], preferred_element_type=F32)

    def pack(one, two):
        return jnp.concatenate([one.reshape(OWNERS, SLOTS, LANES), two.reshape(OWNERS, SLOTS, LANES)],
                               axis=1).astype(BF16)

    load_codes.wait()
    load_vec.wait()
    row8 = lax.broadcasted_iota(I32, (8, LANES), 0)
    list_rows = jnp.where(row8 == 0, list_no >> 8, jnp.where(row8 == 1, list_no & 255, 0)).astype(F32)
    load = jnp.concatenate(
        [codes_v[...].astype(F32), list_rows, jnp.zeros((CODES - 2 * SUBS - 8, LANES), F32)], axis=0).astype(BF16)
    rows = lax.dot_general(place_v[...], load, (((1,), (1,)), ((), ())), preferred_element_type=F32)
    code_out[...] = pack(rows[:, 0:128] + extra(0), rows[:, 128:256] + extra(1))

    load_cent.wait()
    pl.semaphore_wait(barrier, OWNERS - 1 + GROUPS - 1 + 9)

    def code_copy(k):
        peer = nth_peer(k)
        return pltpu.make_async_remote_copy(
            code_out.at[peer], code_in.at[owner], code_send, code_recv, device_id=(group, peer), device_id_type=MESH)

    def vec_copy(k):
        peer = nth_peer(k)
        return pltpu.make_async_remote_copy(
            vec_out.at[peer], vec_in.at[owner], vec_send, vec_recv, device_id=(group, peer), device_id_type=MESH)

    across = []
    for j in range(1, 4):
        across.append(pltpu.make_async_remote_copy(
            table.at[group], table.at[group], x_send.at[j - 1], x_recv.at[j - 1],
            device_id=((group + 2 * j) % GROUPS, owner), device_id_type=MESH))
    aside = [pltpu.make_async_remote_copy(
        table.at[group], table.at[group], sib_send.at[0], sib_recv.at[0],
        device_id=(sibling, owner), device_id_type=MESH)]
    each(0, OWNERS - 1, lambda k: code_copy(k).start())
    for copy in across + aside:
        copy.start()
    code_in[owner] = code_out[owner]

    for p in range(PAIRS):
        rows = jnp.dot(place_v[...], vec_v[:, 256 * p: 256 * p + 256], preferred_element_type=F32)
        vec_out[:, 16 * p: 16 * p + 16, :] = pack(
            rows[:, 0:128] + extra(2 + 2 * p), rows[:, 128:256] + extra(3 + 2 * p))
    vec_in[owner] = vec_out[owner]
    left_half = lax.broadcasted_iota(I32, (WIDTH, LANES), 1) < 64

    def by_code(pairs):
        lefts, rights = [], []
        low_level = lax.broadcasted_iota(I32, (64, pairs[0][1].shape[1]), 0)
        for rows, code in pairs:
            high = code >> 6
            lefts += [jnp.where(high == h, rows, 0.0) for h in range(4)]
            rights.append((low_level == (code & 63)).astype(F32))
        out = lax.dot_general(
            jnp.concatenate(lefts, axis=0).astype(BF16), jnp.concatenate(rights, axis=0).astype(BF16),
            (((1,), (1,)), ((), ())), preferred_element_type=F32)
        results = []
        for q in range(4):
            column = 128 * (q // 2)
            tiles = []
            for t in range(2):
                one = out[32 * q + 16 * t: 32 * q + 16 * t + 8, column: column + 128]
                two = out[32 * q + 16 * t + 8: 32 * q + 16 * t + 16, column: column + 128]
                if q % 2 == 0:
                    two = pltpu.roll(two, 64, 1)
                else:
                    one = pltpu.roll(one, 64, 1)
                tiles.append(jnp.where(left_half, one, two))
            results.append(jnp.concatenate(tiles, axis=1))
        return results

    def pairs_of(chunks):
        return [(ch, mm, r) for ch in chunks for mm in range(CHUNK_SUBS) for r in range(2)]

    ones = jnp.ones((WIDTH, LANES), F32)
    tile_row = lax.broadcasted_iota(I32, (8, CODES), 0)

    def count(c):
        pairs = pairs_of([2 * c, 2 * c + 1])
        tiles = [jnp.zeros((8, CODES), F32)] * 2
        for first in range(0, len(pairs), 4):
            four = pairs[first: first + 4]
            got = by_code([(ones, codes_v[pl.ds(r * SUBS + ch * CHUNK_SUBS + mm, 1), :]) for ch, mm, r in four])
            for n, (ch, mm, r) in enumerate(four):
                at = (first + n) // 6
                tiles[at] = jnp.where(tile_row == r * CHUNK_SUBS + mm, got[n], tiles[at])
        tally[2 * c] = tiles[0]
        tally[2 * c + 1] = tiles[1]

    each(0, CHUNKS // 2, count)

    t_core = pltpu.make_async_remote_copy(
        tally.at[pl.ds((1 - core) * PLANE, PLANE)], tally_half, t_core_send, t_core_recv,
        device_id=(sibling, owner), device_id_type=MESH)
    t_core.start()
    for j in range(6):
        vec_t[128 * j: 128 * j + 128, :] = vec_v[:, 128 * j: 128 * j + 128].astype(F32).T

    def t_plane_copy(k):
        i = plane_to(k)
        return pltpu.make_async_remote_copy(
            tally_plane.at[i], tally_plane_in.at[xy], t_plane_send, t_plane_recv,
            device_id=plane_device(i), device_id_type=MESH)

    def t_line_copy(unit):
        return pltpu.make_async_remote_copy(
            tally_line.at[unit % 2], tally_line_in.at[z], t_line_send.at[unit], t_line_recv,
            device_id=(group, y * 16 + UNIT_PLACES[unit]), device_id_type=MESH)

    def vector_sums(c):
        pairs = pairs_of([2 * c, 2 * c + 1])
        for first in range(0, len(pairs), 4):
            four = pairs[first: first + 4]
            got = by_code([(vec_t[pl.ds(8 * (ch * CHUNK_SUBS + mm), 8), :],
                            codes_v[pl.ds(r * SUBS + ch * CHUNK_SUBS + mm, 1), :]) for ch, mm, r in four])
            for n, (ch, mm, r) in enumerate(four):
                sums[ch, 16 * mm + 8 * r: 16 * mm + 8 * r + 8, :] = got[n]

    def total_of(ref):
        total = ref[0]
        for i in range(1, PLANE):
            total = total + ref[i]
        return total

    each(0, CHUNKS // 4, vector_sums)
    t_core.wait_recv()
    tally_plane[...] = tally[pl.ds(core * PLANE, PLANE)] + tally_half[...]
    each(1, PLANE, lambda k: t_plane_copy(k).start())
    tally_plane_in[xy] = tally_plane[xy]
    for j in range(1, 4):
        source = (group + 2 * GROUPS - 2 * j) % GROUPS
        across[j - 1].wait_recv()
        relay = pltpu.make_async_remote_copy(
            table.at[source], table.at[source], sib_send.at[j], sib_recv.at[j],
            device_id=(sibling, owner), device_id_type=MESH)
        relay.start()
        aside.append(relay)
    each(CHUNKS // 4, CHUNKS // 2, vector_sums)
    wait_bytes(tally_plane.at[pl.ds(0, PLANE - 1)], t_plane_recv)
    total = total_of(tally_plane_in)
    tally_line[0] = total[:, 0:128]
    tally_line[1] = total[:, 128:256]
    for unit, where in enumerate(UNIT_PLACES):
        @pl.when(z != where)
        def _(unit=unit):
            t_line_copy(unit).start()
    each(0, VEC_FIRST, lambda k: vec_copy(k).start())

    wait_bytes(code_in.at[pl.ds(0, OWNERS - 1)], code_recv)

    code_f[...] = code_in[...].astype(F32)
    for h in range(2):
        rows = jnp.concatenate([code_f[:, 8 * h + s, :] for s in range(CAP)], axis=0)
        held_codes[128 * h: 128 * h + 128, :] = rows.T.astype(I32)
        if h == 1:
            which = rows[:, 64:65] * 256.0 + rows[:, 65:66]
    lane = lax.broadcasted_iota(I32, (HELD, LISTS_HERE), 1).astype(F32) + 1.0
    pick_v[...] = (which == lane).astype(F32).astype(BF16)
    for copy in aside:
        copy.wait_recv()
    rows = jnp.dot(pick_v[...], table[...].reshape(LISTS_HERE, DIM), preferred_element_type=F32)
    for j in range(6):
        base_t[128 * j: 128 * j + 128, :] = rows[:, 128 * j: 128 * j + 128].T

    def centroid_sums(chunks):
        pairs = pairs_of(chunks)
        for first in range(0, len(pairs), 4):
            four = pairs[first: first + 4]
            got = by_code([(base_t[pl.ds(8 * (ch * CHUNK_SUBS + mm), 8), :],
                            held_codes[pl.ds(r * SUBS + ch * CHUNK_SUBS + mm, 1), :]) for ch, mm, r in four])
            for n, (ch, mm, r) in enumerate(four):
                sums[ch, 16 * mm + 8 * r: 16 * mm + 8 * r + 8, :] -= got[n]

    def core_copy(k):
        i = plane_to(k + 1)
        return pltpu.make_async_remote_copy(
            sums.at[(1 - core) * PLANE + i], half.at[i], core_send.at[k], core_recv.at[k],
            device_id=(sibling, owner), device_id_type=MESH)

    def plane_copy(k):
        i = plane_to(k + 1)
        return pltpu.make_async_remote_copy(
            plane.at[i], plane_in.at[xy], plane_send, plane_recv, device_id=plane_device(i), device_id_type=MESH)

    def other_half(c):
        k = 2 * c
        centroid_sums([(1 - core) * PLANE + plane_to(k + 1), (1 - core) * PLANE + plane_to(k + 2)])
        core_copy(k).start()
        core_copy(k + 1).start()

    def own_half(c):
        k = 2 * c
        centroid_sums([core * PLANE + plane_to(k + 1), core * PLANE + plane_to(k + 2)])
        for n in (k, k + 1):
            i = plane_to(n + 1)
            core_copy(n).wait_recv()
            plane[i] = sums[core * PLANE + i] + half[i]

            @pl.when(n < PLANE - 1)
            def _(n=n):
                plane_copy(n).start()

    def both_halves(c):
        @pl.when(c < PLANE // 2)
        def _():
            other_half(c)

        @pl.when(c > 0)
        def _():
            own_half(c - 1)

    each(0, PLANE // 2 + 1, both_halves)
    plane_in[xy] = plane[xy]
    wait_bytes(plane.at[pl.ds(0, PLANE - 1)], plane_recv)
    total = total_of(plane_in)
    for unit in range(6):
        mm, side = unit // 2, unit % 2
        line[unit] = total[16 * mm: 16 * mm + 16, 128 * side: 128 * side + 128]

    def line_copy(unit):
        return pltpu.make_async_remote_copy(
            line.at[unit], line_in.at[z], line_send.at[unit], line_recv,
            device_id=(group, y * 16 + UNIT_PLACES[unit]), device_id_type=MESH)

    for unit, where in enumerate(UNIT_PLACES):
        @pl.when(z != where)
        def _(unit=unit):
            line_copy(unit).start()

    each(VEC_FIRST, OWNERS - 1, lambda k: vec_copy(k).start())

    def unit_ref(unit):
        mm, side = unit // 2, unit % 2
        return book_ref.at[chunk, 8 * mm: 8 * mm + 8, 128 * side: 128 * side + 128]

    def unit_copy(unit, k):
        return pltpu.make_async_remote_copy(
            unit_ref(unit), unit_ref(unit), unit_send, unit_recv.at[unit],
            device_id=(group, y * 16 + (z + far_first(k)) % 16), device_id_type=MESH)

    load_book.wait()
    for unit, where in enumerate(UNIT_PLACES):
        mm, side = unit // 2, unit % 2

        @pl.when(z == where)
        def _(unit=unit, mm=mm, side=side, where=where):
            line_in[where] = line[unit]
            tally_line_in[where] = tally_line[side]
            wait_bytes(tally_line_in.at[pl.ds(0, PLANE - 1)], t_line_recv)
            counts = total_of(tally_line_in)
            wait_bytes(line_in.at[pl.ds(0, PLANE - 1)], line_recv)
            total = total_of(line_in)
            here = slice(128 * side, 128 * side + 128)
            start = book0_v[8 * mm: 8 * mm + 8, here]
            first = (total[0:8] + PRIOR * start) / (counts[mm: mm + 1] + PRIOR)
            book_ref[chunk, 8 * mm: 8 * mm + 8, here] = (
                (total[8:16] + PRIOR * first) / (counts[3 + mm: 4 + mm] + PRIOR))
            each(0, PLANE - 1, lambda k: unit_copy(unit, k).start())

    for unit, where in enumerate(UNIT_PLACES):
        @pl.when(z != where)
        def _(unit=unit):
            wait_bytes(unit_ref(unit), unit_recv.at[unit])

    def gather_copy(k):
        return pltpu.make_async_remote_copy(
            book_ref.at[chunk], book_ref.at[chunk], gather_send, gather_recv.at[k],
            device_id=plane_device(plane_to(k)), device_id_type=MESH)

    def back_copy(k):
        part = book_ref.at[core * PLANE + plane_from(k)]
        return pltpu.make_async_remote_copy(
            part, part, back_send, back_recv.at[k], device_id=(sibling, owner), device_id_type=MESH)

    each(1, PLANE, lambda k: gather_copy(k).start())
    back_copy(0).start()

    def take_spare(part):
        for h in range(2):
            for i in range(2):
                t = 2 * (part + h) + i
                spare_f[OWNERS * t: OWNERS * t + OWNERS, :] = code_f[:, 8 * h + 6 + i, :]

    code_f[...] = code_in[...].astype(F32)
    take_spare(0)
    wait_bytes(vec_in.at[pl.ds(0, OWNERS - 1)], vec_recv)
    for p in range(PAIRS):
        code_f[...] = vec_in[:, 16 * p: 16 * p + 16, :].astype(F32)
        take_spare(2 + 2 * p)
        for h in range(2):
            j = 2 * p + h
            rows = jnp.concatenate([code_f[:, 8 * h + s, :] for s in range(CAP)], axis=0)
            base_t[128 * j: 128 * j + 128, :] = rows.T - base_t[128 * j: 128 * j + 128, :]
    for j in range(4, 6):
        rows = spare_f[HELD * (j - 4): HELD * (j - 4) + HELD, :]
        base_t[128 * j: 128 * j + 128, :] = rows.T - base_t[128 * j: 128 * j + 128, :]

    def add(ch, totals):
        for mm in range(CHUNK_SUBS):
            m = ch * CHUNK_SUBS + mm
            left = book_ref[ch, 8 * mm: 8 * mm + 8, 0:128]
            right = book_ref[ch, 8 * mm: 8 * mm + 8, 128:256]
            row = jnp.broadcast_to(held_codes[pl.ds(SUBS + m, 1), :], (WIDTH, HELD))
            rest = base_t[pl.ds(8 * m, 8), :]
            new = []
            for t in range(HELD // LANES):
                code = row[:, 128 * t: 128 * t + 128]
                low = code & 127
                one = jnp.take_along_axis(left, low, axis=1)
                two = jnp.take_along_axis(right, low, axis=1)
                diff = rest[:, 128 * t: 128 * t + 128] - jnp.where(code > 127, two, one)
                new.append(totals[t] + diff * diff)
            totals = tuple(new)
        return totals

    def arrivals(k, totals):
        i = plane_from(k)
        part = book_ref.at[core * PLANE + i]
        wait_bytes(part, gather_recv.at[k])
        back_copy(k).start()
        before_it = (1 - core) * PLANE + plane_from(k - 1)
        wait_bytes(part, back_recv.at[k - 1])
        return add(before_it, add(core * PLANE + i, totals))

    zero = jnp.zeros((WIDTH, LANES), F32)
    totals = add(chunk, (zero,) * 3)
    totals = lax.fori_loop(1, PLANE, arrivals, totals)
    wait_bytes(book_ref.at[0], back_recv.at[PLANE - 1])
    totals = add((1 - core) * PLANE + plane_from(PLANE - 1), totals)
    error = jnp.concatenate([jnp.sum(t, axis=0, keepdims=True) for t in totals], axis=1) / float(DIM)
    top = error.astype(BF16).astype(F32)
    mid = (error - top).astype(BF16).astype(F32)
    low = error - top - mid
    row = lax.broadcasted_iota(I32, (16, HELD), 0)
    split = jnp.where(row == 0, top, jnp.where(row == 1, mid, jnp.where(row == 2, low, 0.0))).astype(BF16)
    by_list = jnp.sum(jnp.dot(split, pick_v[...], preferred_element_type=F32), axis=0, keepdims=True)
    for i in range(GROUPS):
        parts[i] = by_list[:, 128 * i: 128 * i + 128]

    def part_copy(k):
        return pltpu.make_async_remote_copy(
            parts.at[(group + k) % GROUPS], parts_in.at[group], part_send, part_recv,
            device_id=((group + k) % GROUPS, owner), device_id_type=MESH)

    for k in range(1, GROUPS):
        part_copy(k).start()
    parts_in[group] = parts[group]

    t_core.wait_send()
    wait_bytes(tally_plane.at[pl.ds(0, PLANE - 1)], t_plane_send)
    wait_bytes(code_in.at[pl.ds(0, OWNERS - 1)], code_send)
    wait_bytes(vec_in.at[pl.ds(0, OWNERS - 1)], vec_send)
    for copy in across + aside:
        copy.wait_send()
    each(0, PLANE, lambda k: core_copy(k).wait_send())
    wait_bytes(plane.at[pl.ds(0, PLANE - 1)], plane_send)
    for unit, where in enumerate(UNIT_PLACES):
        @pl.when(z != where)
        def _(unit=unit):
            line_copy(unit).wait_send()
            t_line_copy(unit).wait_send()

        @pl.when(z == where)
        def _(unit=unit):
            each(0, PLANE - 1, lambda k: unit_copy(unit, k).wait_send())
    wait_bytes(book_ref.at[pl.ds(0, PLANE - 1)], gather_send)
    wait_bytes(book_ref.at[pl.ds(0, PLANE)], back_send)

    wait_bytes(parts.at[pl.ds(0, GROUPS - 1)], part_recv)
    sum_here = parts_in[0]
    for i in range(1, GROUPS):
        sum_here = sum_here + parts_in[i]
    out_ref[...] = sum_here
    wait_bytes(parts.at[pl.ds(0, GROUPS - 1)], part_send)


def local(vectors, list_ids, codes, centroids, codebook0):
    dma = pltpu.SemaphoreType.DMA
    any_place = pl.BlockSpec(memory_space=pltpu.HBM)
    book, list_error = pl.pallas_call(
        index_kernel,
        out_shape=(jax.ShapeDtypeStruct((CHUNKS, CHUNK_SUBS * WIDTH, CODES), F32),
                   jax.ShapeDtypeStruct((1, LANES), F32)),
        in_specs=[any_place] * 5,
        out_specs=(vmem(), vmem()),
        scratch_shapes=[
            pltpu.VMEM((1, LANES), I32),
            pltpu.VMEM((ROWS, DIM), BF16),
            pltpu.VMEM((2 * SUBS, LANES), I32),
            pltpu.VMEM((CHUNK_SUBS * WIDTH, CODES), F32),
            pltpu.VMEM((GROUPS, ROWS, DIM), BF16),
            pltpu.VMEM((OWNERS * SLOTS, LANES), BF16),
            pltpu.VMEM((3, OWNERS * SLOTS, LANES), BF16),
            pltpu.VMEM((DIM, LANES), F32),
            pltpu.VMEM((OWNERS, 16 * PAIRS, LANES), BF16),
            pltpu.VMEM((OWNERS, 16 * PAIRS, LANES), BF16),
            pltpu.VMEM((OWNERS, 16, LANES), BF16),
            pltpu.VMEM((OWNERS, 16, LANES), BF16),
            pltpu.VMEM((OWNERS, 16, LANES), F32),
            pltpu.VMEM((2 * HELD, LANES), F32),
            pltpu.VMEM((CODES, HELD), I32),
            pltpu.VMEM((HELD, LISTS_HERE), BF16),
            pltpu.VMEM((DIM, HELD), F32),
            pltpu.VMEM((CHUNKS, CHUNK_ROWS, CODES), F32),
            pltpu.VMEM((PLANE, CHUNK_ROWS, CODES), F32),
            pltpu.VMEM((PLANE, CHUNK_ROWS, CODES), F32),
            pltpu.VMEM((PLANE, CHUNK_ROWS, CODES), F32),
            pltpu.VMEM((6, 16, LANES), F32),
            pltpu.VMEM((PLANE, 16, LANES), F32),
            pltpu.VMEM((GROUPS, 1, LANES), F32),
            pltpu.VMEM((GROUPS, 1, LANES), F32),
            pltpu.VMEM((CHUNKS, 8, CODES), F32),
            pltpu.VMEM((PLANE, 8, CODES), F32),
            pltpu.VMEM((PLANE, 8, CODES), F32),
            pltpu.VMEM((PLANE, 8, CODES), F32),
            pltpu.VMEM((2, 8, LANES), F32),
            pltpu.VMEM((PLANE, 8, LANES), F32),
            dma((5,)),
            dma, dma, dma, dma,
            dma((3,)), dma((3,)), dma((4,)), dma((4,)),
            dma((PLANE,)), dma((PLANE,)),
            dma, dma,
            dma((6,)), dma,
            dma, dma((6,)),
            dma, dma((PLANE,)), dma, dma((PLANE,)), dma, dma,
            dma, dma, dma, dma, dma((6,)), dma,
        ],
        compiler_params=pltpu.CompilerParams(collective_id=0, has_side_effects=True, vmem_limit_bytes=VMEM_LIMIT),
    )(list_ids.reshape(1, ROWS), vectors, codes, centroids,
      codebook0.reshape(CHUNKS, CHUNK_SUBS * WIDTH, CODES))
    return book.reshape(SUBS, WIDTH, CODES), list_error.reshape(ROWS)


def solution(mesh):
    in_specs = (
        P(("groups", "owners"), None),
        P(("groups", "owners")),
        P(None, ("groups", "owners")),
        P(("groups", "owners"), None),
        P(),
    )
    out_specs = (P(), P(("groups", "owners")))
    return jax.shard_map(local, mesh=mesh, in_specs=in_specs, out_specs=out_specs, check_vma=False)
```

time: 105 us -> 89.3 us (0.85)
  Pallas kernels: 98.7 us -> 85.9 us
  local copies, waits for them, and re-layouts: 5.92 us -> 2.58 us
    pallas_call x1, Pallas kernels: 98.7 us -> 85.9 us  [local(): pl.pallas_call(index_kernel, out_shape=(jax.ShapeDtypeStruct((CHUNKS, CHU...]
    unnamed x12 -> x4, local copies, waits for them, and re-layouts: 5.92 us -> 2.58 us
where the time goes in v3:
time: 89.3 us; the launch traced here: 89.1 us
  Pallas kernels  85.9 us (96%)
  local copies, waits for them, and re-layouts  2.58 us (3%)
    pallas_call x1, Pallas kernels, local(): pl.pallas_call(index_kernel, out_shape=(jax.ShapeDtypeStruct((CHUNKS, CHU...  85.9 us
    unnamed x4, local copies, waits for them, and re-layouts  2.58 us

profile of v3, /device:TPU:1, one launch (start us, length us, event | category | flops | bytes accessed | tf_op | source)
XLA Modules:
  0.0 89.1 jit_solution(11343292048642111934)
XLA Ops:
  0.6 85.9 %shard_map.68 = (f32[32,24,256]{2,1,0:T(8,128)}, f32[1,128]{1,0:T(1,128)}) custom-call(s32[1,128]{1,0:T(1,128)} %bitcast.6, bf16[128,768]{1,0:T(8,128)(2,1)} %vec_hbm.1, s32[192,128]{1,0:T(8,128)} %codes_hbm.1, bf16[128,768]{1,0:T(8,128)(2,1)} %cent_hbm.1, f32[32,24,256]{2,1,0:T(8,128)} %bitcast.4), custom_call_target="tpu_custom_call" | custom-call | tf_op jit(solution)/shard_map/pallas_call | solution.py:508
  86.5 0.0 copy-start
  86.6 2.1 %copy.9 = f32[96,8,256]{2,1,0:T(8,128)} copy(f32[96,8,256]{2,1,0:T(8,128)} %bitcast.5) | data formatting | bytes 1572864
  88.6 0.0 copy-done
  88.6 0.5 copy.10
Async XLA Ops:
  86.5 2.1 %copy-start = (f32[1,128]{1,0:T(1,128)S(1)}, f32[1,128]{1,0:T(1,128)}, u32[]{:S(2)}) copy-start(f32[1,128]{1,0:T(1,128)} %get-tuple-element.5) | copy-start | bytes 1540

commit v4 on v3

--- a/solution.py
+++ b/solution.py
@@ -28,9 +28,9 @@
 PLANE = 16
 PRIOR = 128.0
 UNIT_PLACES = (0, 2, 5, 8, 10, 13)
-VEC_FIRST = 28
+VEC_FIRST = 7
 HELD = CAP * OWNERS
-VMEM_LIMIT = 60 * 1024 * 1024
+VMEM_LIMIT = 48 * 1024 * 1024
 
 
 def vmem():
@@ -60,10 +60,10 @@
 
 
 def index_kernel(ids_hbm, vec_hbm, codes_hbm, cent_hbm, book0_hbm, book_ref, out_ref,
-                 ids_v, vec_v, codes_v, book0_v, table, place_v, spare_v, vec_t, vec_out, vec_in, code_out, code_in,
+                 ids_v, vec_v, codes_v, book0_v, table, place_v, spare_v, vec_t, vec_out, vec_mid, vec_in, code_out, code_in,
                  code_f, spare_f, held_codes, pick_v, base_t, sums, half, plane, plane_in, line, line_in, parts, parts_in,
                  tally, tally_half, tally_plane, tally_plane_in, tally_line, tally_line_in,
-                 load_sem, code_send, code_recv, vec_send, vec_recv, x_send, x_recv, sib_send, sib_recv,
+                 load_sem, code_send, code_recv, row_send, row_recv, vec_send, vec_recv, x_send, x_recv, sib_send, sib_recv,
                  core_send, core_recv, plane_send, plane_recv, line_send, line_recv,
                  unit_send, unit_recv, gather_send, gather_recv, back_send, back_recv, part_send, part_recv,
                  t_core_send, t_core_recv, t_plane_send, t_plane_recv, t_line_send, t_line_recv):
@@ -147,10 +147,15 @@
         return pltpu.make_async_remote_copy(
             code_out.at[peer], code_in.at[owner], code_send, code_recv, device_id=(group, peer), device_id_type=MESH)
 
+    def row_copy(j):
+        to = (y + j) % 4
+        return pltpu.make_async_remote_copy(
+            vec_out.at[to], vec_mid.at[y], row_send, row_recv, device_id=(group, to * 16 + z), device_id_type=MESH)
+
     def vec_copy(k):
-        peer = nth_peer(k)
-        return pltpu.make_async_remote_copy(
-            vec_out.at[peer], vec_in.at[owner], vec_send, vec_recv, device_id=(group, peer), device_id_type=MESH)
+        to = (z + far_first(k)) % 16
+        return pltpu.make_async_remote_copy(
+            vec_mid.at[:, to], vec_in.at[:, z], vec_send, vec_recv, device_id=(group, y * 16 + to), device_id_type=MESH)
 
     across = []
     for j in range(1, 4):
@@ -167,9 +172,11 @@
 
     for p in range(PAIRS):
         rows = jnp.dot(place_v[...], vec_v[:, 256 * p: 256 * p + 256], preferred_element_type=F32)
-        vec_out[:, 16 * p: 16 * p + 16, :] = pack(
-            rows[:, 0:128] + extra(2 + 2 * p), rows[:, 128:256] + extra(3 + 2 * p))
-    vec_in[owner] = vec_out[owner]
+        vec_out[:, :, 16 * p: 16 * p + 16, :] = pack(
+            rows[:, 0:128] + extra(2 + 2 * p), rows[:, 128:256] + extra(3 + 2 * p)).reshape(4, 16, 16, LANES)
+    for j in (2, 1, 3):
+        row_copy(j).start()
+    vec_mid[y] = vec_out[y]
     left_half = lax.broadcasted_iota(I32, (WIDTH, LANES), 1) < 64
 
     def by_code(pairs):
@@ -272,7 +279,9 @@
         @pl.when(z != where)
         def _(unit=unit):
             t_line_copy(unit).start()
+    wait_bytes(vec_mid.at[pl.ds(0, 3)], row_recv)
     each(0, VEC_FIRST, lambda k: vec_copy(k).start())
+    vec_in[:, pl.ds(z, 1)] = vec_mid[:, pl.ds(z, 1)]
 
     wait_bytes(code_in.at[pl.ds(0, OWNERS - 1)], code_recv)
 
@@ -355,7 +364,7 @@
         def _(unit=unit):
             line_copy(unit).start()
 
-    each(VEC_FIRST, OWNERS - 1, lambda k: vec_copy(k).start())
+    each(VEC_FIRST, PLANE - 1, lambda k: vec_copy(k).start())
 
     def unit_ref(unit):
         mm, side = unit // 2, unit % 2
@@ -411,9 +420,9 @@
 
     code_f[...] = code_in[...].astype(F32)
     take_spare(0)
-    wait_bytes(vec_in.at[pl.ds(0, OWNERS - 1)], vec_recv)
+    wait_bytes(vec_in.at[:, pl.ds(0, PLANE - 1)], vec_recv)
     for p in range(PAIRS):
-        code_f[...] = vec_in[:, 16 * p: 16 * p + 16, :].astype(F32)
+        code_f[...] = vec_in[:, :, 16 * p: 16 * p + 16, :].reshape(OWNERS, 16, LANES).astype(F32)
         take_spare(2 + 2 * p)
         for h in range(2):
             j = 2 * p + h
@@ -477,7 +486,8 @@
     t_core.wait_send()
     wait_bytes(tally_plane.at[pl.ds(0, PLANE - 1)], t_plane_send)
     wait_bytes(code_in.at[pl.ds(0, OWNERS - 1)], code_send)
-    wait_bytes(vec_in.at[pl.ds(0, OWNERS - 1)], vec_send)
+    wait_bytes(vec_mid.at[pl.ds(0, 3)], row_send)
+    wait_bytes(vec_in.at[:, pl.ds(0, PLANE - 1)], vec_send)
     for copy in across + aside:
         copy.wait_send()
     each(0, PLANE, lambda k: core_copy(k).wait_send())
@@ -520,8 +530,9 @@
             pltpu.VMEM((OWNERS * SLOTS, LANES), BF16),
             pltpu.VMEM((3, OWNERS * SLOTS, LANES), BF16),
             pltpu.VMEM((DIM, LANES), F32),
-            pltpu.VMEM((OWNERS, 16 * PAIRS, LANES), BF16),
-            pltpu.VMEM((OWNERS, 16 * PAIRS, LANES), BF16),
+            pltpu.VMEM((4, 16, 16 * PAIRS, LANES), BF16),
+            pltpu.VMEM((4, 16, 16 * PAIRS, LANES), BF16),
+            pltpu.VMEM((4, 16, 16 * PAIRS, LANES), BF16),
             pltpu.VMEM((OWNERS, 16, LANES), BF16),
             pltpu.VMEM((OWNERS, 16, LANES), BF16),
             pltpu.VMEM((OWNERS, 16, LANES), F32),
@@ -544,7 +555,7 @@
             pltpu.VMEM((2, 8, LANES), F32),
             pltpu.VMEM((PLANE, 8, LANES), F32),
             dma((5,)),
-            dma, dma, dma, dma,
+            dma, dma, dma, dma, dma, dma,
             dma((3,)), dma((3,)), dma((4,)), dma((4,)),
             dma((PLANE,)), dma((PLANE,)),
             dma, dma,
@@ -554,8 +565,9 @@
             dma, dma, dma, dma, dma((6,)), dma,
         ],
         compiler_params=pltpu.CompilerParams(collective_id=0, has_side_effects=True, vmem_limit_bytes=VMEM_LIMIT),
-    )(list_ids.reshape(1, ROWS), vectors, codes, centroids,
-      codebook0.reshape(CHUNKS, CHUNK_SUBS * WIDTH, CODES))
+    )(*[pltpu.with_memory_space_constraint(ref, pltpu.HBM) for ref in (
+        list_ids.reshape(1, ROWS), vectors, codes, centroids,
+        codebook0.reshape(CHUNKS, CHUNK_SUBS * WIDTH, CODES))])
     return book.reshape(SUBS, WIDTH, CODES), list_error.reshape(ROWS)
 
 

time: 89.3 us -> 85.3 us (0.955)
  Pallas kernels: 85.9 us -> 83.1 us
  local copies, waits for them, and re-layouts: 2.58 us -> 1.39 us
    pallas_call x1, Pallas kernels: 85.9 us -> 83.1 us  [local(): pl.pallas_call(index_kernel, out_shape=(jax.ShapeDtypeStruct((CHUNKS, CHU...]
    unnamed x4 -> x2, local copies, waits for them, and re-layouts: 2.58 us -> 1.39 us
where the time goes in v4:
time: 85.3 us; the launch traced here: 85.2 us
  Pallas kernels  83.1 us (97%)
  local copies, waits for them, and re-layouts  1.39 us (2%)
    pallas_call x1, Pallas kernels, local(): pl.pallas_call(index_kernel, out_shape=(jax.ShapeDtypeStruct((CHUNKS, CHU...  83.1 us

profile of v4, /device:TPU:1, one launch (start us, length us, event | category | flops | bytes accessed | tf_op | source)
XLA Modules:
  0.0 85.2 jit_solution(11736772457600660701)
XLA Ops:
  0.6 83.1 %shard_map.68 = (f32[32,24,256]{2,1,0:T(8,128)S(1)}, f32[1,128]{1,0:T(1,128)S(1)}) custom-call(s32[1,128]{1,0:T(1,128)} %bitcast.7, bf16[128,768]{1,0:T(8,128)(2,1)} %vec_hbm.1, s32[192,128]{1,0:T(8,128)} %codes_hbm.1, bf16[128,768]{1,0:T(8,128)(2,1)} %cent_hbm.1, f32[32,24,256]{2,1,0:T(8,128)} %bitcast.6), custom_call_target="tpu_custom_call" | custom-call | tf_op jit(solution)/shard_map/pallas_call | solution.py:518
  83.8 0.9 %copy.9 = f32[96,8,256]{2,1,0:T(8,128)} copy(f32[96,8,256]{2,1,0:T(8,128)S(1)} %bitcast.4) | data formatting | bytes 1572864
  84.6 0.5 copy.10

commit v5 on v4

--- a/solution.py
+++ b/solution.py
@@ -75,18 +75,18 @@
     chunk = core * PLANE + xy
 
     def plane_device(i):
-        return ((i // 4) * 2 + core, (i % 4) * 16 + z)
+        return (lax.div(i, 4) * 2 + core, lax.rem(i, 4) * 16 + z)
 
     def plane_to(k):
-        step = (7 * k) % PLANE
-        return (x + step // 4) % 4 * 4 + (y + step % 4) % 4
+        step = lax.rem(7 * k, PLANE)
+        return lax.rem(x + lax.div(step, 4), 4) * 4 + lax.rem(y + lax.rem(step, 4), 4)
 
     def plane_from(k):
-        step = (7 * k) % PLANE
-        return (x + 4 - step // 4) % 4 * 4 + (y + 4 - step % 4) % 4
+        step = lax.rem(7 * k, PLANE)
+        return lax.rem(x + 4 - lax.div(step, 4), 4) * 4 + lax.rem(y + 4 - lax.rem(step, 4), 4)
 
     def far_first(j):
-        return (8 + (1 - 2 * (j % 2)) * ((j + 1) // 2)) % 16
+        return lax.rem(8 + (1 - 2 * lax.rem(j, 2)) * lax.div(j + 1, 2), 16)
 
     load_ids = local_copy(ids_hbm, ids_v, load_sem.at[0])
     load_codes = local_copy(codes_hbm, codes_v, load_sem.at[1])
@@ -97,7 +97,7 @@
     barrier = pltpu.get_barrier_semaphore()
 
     def nth_peer(k):
-        return (y + 3 - k % 4) % 4 * 16 + (z + far_first(k // 4)) % 16
+        return lax.rem(y + 3 - lax.rem(k, 4), 4) * 16 + lax.rem(z + far_first(lax.div(k, 4)), 16)
 
     each(0, OWNERS - 1, lambda k: pl.semaphore_signal(
         barrier, inc=1, device_id=(group, nth_peer(k)), device_id_type=MESH))
@@ -153,7 +153,7 @@
             vec_out.at[to], vec_mid.at[y], row_send, row_recv, device_id=(group, to * 16 + z), device_id_type=MESH)
 
     def vec_copy(k):
-        to = (z + far_first(k)) % 16
+        to = lax.rem(z + far_first(k), 16)
         return pltpu.make_async_remote_copy(
             vec_mid.at[:, to], vec_in.at[:, z], vec_send, vec_recv, device_id=(group, y * 16 + to), device_id_type=MESH)
 

time: 85.3 us -> 84.4 us (0.989)
  Pallas kernels: 83.1 us -> 82.2 us
    pallas_call x1, Pallas kernels: 83.1 us -> 82.2 us  [local(): pl.pallas_call(index_kernel, out_shape=(jax.ShapeDtypeStruct((CHUNKS, CHU...]
where the time goes in v5:
time: 84.4 us; the launch traced here: 84.3 us
  Pallas kernels  82.2 us (97%)
  local copies, waits for them, and re-layouts  1.39 us (2%)
    pallas_call x1, Pallas kernels, local(): pl.pallas_call(index_kernel, out_shape=(jax.ShapeDtypeStruct((CHUNKS, CHU...  82.2 us

profile of v5, /device:TPU:1, one launch (start us, length us, event | category | flops | bytes accessed | tf_op | source)
XLA Modules:
  0.0 84.3 jit_solution(6109482753326985986)
XLA Ops:
  0.6 82.2 %shard_map.68 = (f32[32,24,256]{2,1,0:T(8,128)S(1)}, f32[1,128]{1,0:T(1,128)S(1)}) custom-call(s32[1,128]{1,0:T(1,128)} %bitcast.7, bf16[128,768]{1,0:T(8,128)(2,1)} %vec_hbm.1, s32[192,128]{1,0:T(8,128)} %codes_hbm.1, bf16[128,768]{1,0:T(8,128)(2,1)} %cent_hbm.1, f32[32,24,256]{2,1,0:T(8,128)} %bitcast.6), custom_call_target="tpu_custom_call" | custom-call | tf_op jit(solution)/shard_map/pallas_call | solution.py:518
  82.9 0.9 %copy.9 = f32[96,8,256]{2,1,0:T(8,128)} copy(f32[96,8,256]{2,1,0:T(8,128)S(1)} %bitcast.4) | data formatting | bytes 1572864
  83.8 0.5 copy.10
